TPU v7x, 256 devices: a whole 4x4x8 slice. The times are simulated.
256 devices in a mesh: lat: 8 (over y_lo, x), lon: 32 (over y_hi, z, core).
Axes of the slice: x: 4, y: 4 (y_hi: 2, y_lo: 2; y = y_hi * 2 + y_lo), z: 8, core: 2. Of those that a mesh axis runs over, the one named last changes fastest.
Arguments:
- latent_field: bfloat16 [48, 384, 4, 512], P('lat', 'lon'), may hold values from -6 to 6
- gain_win: float32 [512], replicated, may hold values from 0.1 to 1.9
- w_qkv_win: bfloat16 [512, 1536], replicated, may hold values from -24 to 24
- w_out_win: bfloat16 [512, 512], replicated, may hold values from -0.25 to 0.25
- gain_shift: float32 [512], replicated, may hold values from 0.1 to 1.9
- w_qkv_shift: bfloat16 [512, 1536], replicated, may hold values from -24 to 24
- w_out_shift: bfloat16 [512, 512], replicated, may hold values from -0.25 to 0.25
- gain_mlp: float32 [512], replicated, may hold values from 0.1 to 1.9
- w_up: bfloat16 [512, 2048], replicated, may hold values from -0.25 to 0.25
- w_down: bfloat16 [2048, 512], replicated, may hold values from -0.125 to 0.125
- gain_merge: float32 [2048], replicated, may hold values from 0.1 to 1.9
- w_merge: bfloat16 [2048, 1024], replicated, may hold values from -0.125 to 0.125
Outputs:
- merged: bfloat16 [24, 192, 4, 1024], P('lat', 'lon')
All inputs are finite; a program needn't handle non-finite values.
Results may differ from a plain program's by a relative error of at most 0.017.
Values may be sent and summed in bfloat16 or wider, within the bound.
No kernel may reach another device: no remote copies, remote signals or barrier semaphores. Data moves between devices by JAX's collectives and lax.ppermute only.
A program may use at most 128 MiB of HBM per device.

v0:
```python
import math

import jax
import jax.numpy as jnp
from jax import lax
from jax.sharding import PartitionSpec as P

HEADS = 16
HEAD = 32
WLAT = 6
WLON = 12
WLEV = 2


epsilon = 1e-05


def passed_along(value, axis, steps):
    count = lax.axis_size(axis)
    pairs = [(source, (source + steps) % count) for source in range(count)]
    return lax.ppermute(value, axis, pairs)


def layer_norm(values, gain_vec):
    values = values.astype(jnp.float32)
    centered = values - jnp.mean(values, axis=-1, keepdims=True)
    spread = jnp.mean(centered * centered, axis=-1, keepdims=True)
    return centered * lax.rsqrt(spread + epsilon) * gain_vec


def to_windows(grid_values):
    row_count, col_count, level_count, channels = grid_values.shape
    blocked = grid_values.reshape(
        row_count // WLAT, WLAT, col_count // WLON, WLON, level_count // WLEV, WLEV, channels
    )
    blocked = blocked.transpose(0, 2, 4, 1, 3, 5, 6)
    return blocked.reshape(-1, WLAT * WLON * WLEV, channels)


def from_windows(windows, row_count, col_count, level_count):
    channels = windows.shape[-1]
    blocked = windows.reshape(
        row_count // WLAT, col_count // WLON, level_count // WLEV, WLAT, WLON, WLEV, channels
    )
    blocked = blocked.transpose(0, 3, 1, 4, 2, 5, 6)
    return blocked.reshape(row_count, col_count, level_count, channels)


def window_attention(normed, labels, w_qkv, w_out, level_offset):
    row_count, col_count, level_count, width = normed.shape
    if level_offset:
        normed = jnp.roll(normed, -level_offset, axis=2)
    windows = to_windows(normed)
    win_count, win_size = (windows.shape[0], windows.shape[1])
    projected = jnp.dot(
        windows.reshape(win_count * win_size, width), w_qkv, preferred_element_type=jnp.float32
    ).astype(jnp.bfloat16)
    projected = projected.reshape(win_count, win_size, 3, HEADS, HEAD)
    scores = jnp.einsum(
        "wshd,wthd->whst",
        projected[:, :, 0],
        projected[:, :, 1],
        preferred_element_type=jnp.float32,
    ) * (1.0 / math.sqrt(HEAD))
    window_labels = to_windows(labels[..., None])[..., 0]
    allowed = (window_labels[:, :, None] == window_labels[:, None, :])[:, None]
    scores = jnp.where(allowed, scores, jnp.float32(-1e30))
    row_max = jnp.max(scores, axis=-1, keepdims=True)
    weights = jnp.exp(scores - row_max)
    probabilities = (weights / jnp.sum(weights, axis=-1, keepdims=True)).astype(jnp.bfloat16)
    context = jnp.einsum(
        "whst,wthd->wshd", probabilities, projected[:, :, 2], preferred_element_type=jnp.float32
    ).astype(jnp.bfloat16)
    context = from_windows(
        context.reshape(win_count, win_size, width), row_count, col_count, level_count
    )
    if level_offset:
        context = jnp.roll(context, level_offset, axis=2)
    projection = jnp.dot(context.reshape(-1, width), w_out, preferred_element_type=jnp.float32)
    return projection.reshape(row_count, col_count, level_count, width)


def shifted_branch(block, row_start, total_lat, gain_vec, w_qkv, w_out):
    half_lat, half_lev = (WLAT // 2, WLEV // 2)
    row_count, col_count, level_count = (block.shape[0], block.shape[1], block.shape[2])
    rolled_rows = (row_start + jnp.arange(row_count)) % total_lat
    lat_label = (rolled_rows >= total_lat - half_lat).astype(jnp.int32)
    lev_label = (jnp.arange(level_count) >= level_count - half_lev).astype(jnp.int32)
    labels = (
        2 * lat_label[:, None, None]
        + lev_label[None, None, :]
        + jnp.zeros((row_count, col_count, level_count), jnp.int32)
    )
    normed = layer_norm(block, gain_vec).astype(jnp.bfloat16)
    return window_attention(normed, labels, w_qkv, w_out, half_lev).astype(jnp.bfloat16)


def merge_patches(grid_values, gain_vec, weight):
    row_count, col_count, level_count, channels = grid_values.shape
    blocked = grid_values.reshape(row_count // 2, 2, col_count // 2, 2, level_count, channels)
    pieces = [blocked[:, index % 2, :, index // 2].astype(jnp.float32) for index in range(4)]
    total = 4 * channels
    mean_all = sum((jnp.sum(piece, axis=-1, keepdims=True) for piece in pieces)) / total
    centered = [piece - mean_all for piece in pieces]
    spread = sum((jnp.sum(entry * entry, axis=-1, keepdims=True) for entry in centered)) / total
    scale_all = lax.rsqrt(spread + epsilon)
    result = None
    for index in range(4):
        normed = (
            centered[index] * scale_all * gain_vec[index * channels : (index + 1) * channels]
        ).astype(jnp.bfloat16)
        term = jnp.dot(
            normed.reshape(-1, channels),
            weight[index * channels : (index + 1) * channels],
            preferred_element_type=jnp.float32,
        )
        result = term if result is None else result + term
    return result.reshape(row_count // 2, col_count // 2, level_count, 2 * channels).astype(
        jnp.bfloat16
    )


def on_device(
    latent_field,
    gain_win,
    w_qkv_win,
    w_out_win,
    gain_shift,
    w_qkv_shift,
    w_out_shift,
    gain_mlp,
    w_up,
    w_down,
    gain_merge,
    w_merge,
):
    row_count, col_count, level_count, width = latent_field.shape
    half_lat, half_lon = (WLAT // 2, WLON // 2)
    total_lat = row_count * lax.axis_size("lat")
    band_index = lax.axis_index("lat")
    zero_labels = jnp.zeros((row_count, col_count, level_count), jnp.int32)
    normed = layer_norm(latent_field, gain_win).astype(jnp.bfloat16)
    after_window = (
        latent_field.astype(jnp.float32)
        + window_attention(normed, zero_labels, w_qkv_win, w_out_win, 0)
    ).astype(jnp.bfloat16)
    eastward = passed_along(after_window[:, :half_lon], "lon", -1)
    widened = jnp.concatenate([after_window[:, half_lon:], eastward], axis=1)
    southern = passed_along(widened[:half_lat], "lat", -1)
    shifted_block = jnp.concatenate([widened[half_lat:], southern], axis=0)
    branch = shifted_branch(
        shifted_block, band_index * row_count, total_lat, gain_shift, w_qkv_shift, w_out_shift
    )
    northern = passed_along(branch[row_count - half_lat :], "lat", 1)
    stacked = jnp.concatenate([northern, branch[: row_count - half_lat]], axis=0)
    westward = passed_along(stacked[:, col_count - half_lon :], "lon", 1)
    branch = jnp.concatenate([westward, stacked[:, : col_count - half_lon]], axis=1)
    after_shift = (after_window.astype(jnp.float32) + branch.astype(jnp.float32)).astype(
        jnp.bfloat16
    )
    normed = layer_norm(after_shift, gain_mlp).astype(jnp.bfloat16).reshape(-1, width)
    hidden = jax.nn.gelu(jnp.dot(normed, w_up, preferred_element_type=jnp.float32)).astype(
        jnp.bfloat16
    )
    down = jnp.dot(hidden, w_down, preferred_element_type=jnp.float32).reshape(after_shift.shape)
    after_mlp = (after_shift.astype(jnp.float32) + down).astype(jnp.bfloat16)
    return merge_patches(after_mlp, gain_merge, w_merge)


def solution(mesh):
    in_specs = (P("lat", "lon", None, None), P(), P(), P(), P(), P(), P(), P(), P(), P(), P(), P())
    out_specs = P("lat", "lon", None, None)
    return jax.shard_map(
        on_device, mesh=mesh, in_specs=in_specs, out_specs=out_specs, check_vma=False
    )
```

profile of v0, /device:TPU:6, one launch (start us, length us, event | category | flops | bytes accessed | tf_op | source)
XLA Modules:
  0.0 101.5 jit_solution(17160866940719084195)
XLA Ops:
  0.0 1.2 %convert_reduce_fusion.1 = f32[6,12,4]{1,2,0:T(4,128)S(1)} fusion(bf16[6,12,4,512]{3,2,1,0:T(4,128)(2,1)} %param.12), kind=kLoop, calls=%fused_computation.38 | loop fusion | flops 294624 | bytes 296064 | tf_op jit(solution)/shard_map/reduce_sum | solution.py:26
  1.3 1.2 %fusion.44 = f32[6,12,4]{1,2,0:T(4,128)S(1)} fusion(bf16[6,12,4,512]{3,2,1,0:T(4,128)(2,1)} %param.12, f32[6,12,4]{1,2,0:T(4,128)S(1)} %broadcast_multiply_fusion.2), kind=kLoop, calls=%fused_computation.61 | loop fusion | flops 589536 | bytes 297216 | tf_op jit(solution)/shard_map/reduce_sum | solution.py:27
  2.5 1.2 %fusion.46 = bf16[6,12,4,512]{3,1,2,0:T(8,128)(2,1)S(1)} fusion(bf16[6,12,4,512]{3,2,1,0:T(4,128)(2,1)} %param.12, f32[512]{0:T(512)} %param.13, f32[6,12,4]{1,2,0:T(4,128)S(1)} %add_rsqrt_fusion.3, f32[6,12,4]{1,2,0:T(4,128)S(1)} %broadcast_multiply_fusion.2), kind=kLoop, calls=%fused_computation.63 | loop fusion | flops 737280 | bytes 594176 | tf_op jit(solution)/shard_map/convert_element_type | solution.py:142
  4.1 3.0 %convolution_convert_fusion.1 = bf16[288,1536]{1,0:T(8,128)(2,1)} fusion(bf16[288,512]{1,0:T(8,128)(2,1)S(1)} %reshape_reshape.13, bf16[512,1536]{1,0:T(8,128)(2,1)} %param.14), kind=kOutput, calls=%fused_computation.12 | convolution fusion | flops 453427200 | bytes 2752512 | tf_op jit(solution)/shard_map/dot_general | solution.py:55
  7.1 1.6 %copy.51 = bf16[288,1536]{0,1:T(8,128)(2,1)S(1)} copy(bf16[288,1536]{1,0:T(8,128)(2,1)} %convolution_convert_fusion.1) | data formatting | bytes 1769472 | tf_op jit(solution)/shard_map/convert_element_type | solution.py:57
  8.8 1.5 %reshape.225 = bf16[2,144,3,16,32]{1,0,4,3,2:T(2,128)(2,1)} reshape(bf16[288,1536]{0,1:T(8,128)(2,1)S(1)} %copy.51) | data formatting | bytes 1769472 | tf_op jit(solution)/shard_map/reshape | solution.py:58
  10.2 2.5 %fusion.96 = (bf16[2,144,1,16,32]{1,0,4,3,2:T(2,128)(2,1)S(1)}, bf16[2,144,1,16,32]{1,0,4,3,2:T(2,128)(2,1)S(1)}, bf16[2,144,1,16,32]{1,0,4,3,2:T(2,128)(2,1)S(1)}) fusion(bf16[2,144,3,16,32]{1,0,4,3,2:T(2,128)(2,1)} %reshape.225), kind=kLoop, calls=%fused_computation.156 | loop fusion | bytes 1769472 | tf_op jit(solution)/shard_map/slice | solution.py:72
  13.6 4.5 %fusion.100 = (f32[2,16,144]{2,1,0:T(8,128)S(1)}, f32[2,16,144,144]{2,3,1,0:T(8,128)S(1)}) fusion(f32[2,16,144,144]{2,3,1,0:T(8,128)S(1)} %fusion.51), kind=kOutput, calls=%fused_computation.160 | output fusion | flops 2654351 | bytes 5326848 | tf_op jit(solution)/shard_map/sub | solution.py:69
  18.1 1.2 %fusion.23 = bf16[2,144,16,32]{1,3,2,0:T(8,128)(2,1)} fusion(f32[2,16,144,144]{2,3,1,0:T(8,128)S(1)} %get-tuple-element.36, f32[2,16,144]{2,1,0:T(8,128)S(1)} %get-tuple-element.35, bf16[2,144,1,16,32]{1,0,4,3,2:T(2,128)(2,1)S(1)} %get-tuple-element.18), kind=kOutput, calls=%fused_computation.32 | convolution fusion | flops 43941888 | bytes 3262464 | tf_op jit(solution)/shard_map/whst,wthd->wshd/dot_general | solution.py:71
  19.4 1.9 %copy.56 = bf16[2,144,16,32]{3,2,1,0:T(8,128)(2,1)S(1)} copy(bf16[2,144,16,32]{1,3,2,0:T(8,128)(2,1)} %fusion.23) | data formatting | bytes 589824 | tf_op jit(solution)/shard_map/convert_element_type | solution.py:73
  21.3 1.6 %reshape_reshape.14 = bf16[1,1,2,6,12,2,512]{6,5,4,3,2,1,0:T(2,128)(2,1)} reshape(bf16[2,144,16,32]{3,2,1,0:T(8,128)(2,1)S(1)} %copy.56) | data formatting | bytes 589824 | tf_op jit(solution)/shard_map/reshape;reshape | solution.py:42
  24.0 1.5 %fusion.22 = bf16[6,12,4,512]{3,1,2,0:T(8,128)(2,1)S(1)} fusion(bf16[6,12,4,512]{3,1,2,0:T(8,128)(2,1)S(1)} %bitcast.137, bf16[512,512]{1,0:T(8,128)(2,1)} %param.15, bf16[6,12,4,512]{3,2,1,0:T(4,128)(2,1)} %param.12), kind=kOutput, calls=%fused_computation.30 | convolution fusion | flops 151437312 | bytes 1409024 | tf_op jit(solution)/shard_map/dot_general | solution.py:79
  26.3 8.0 %collective-permute-start = (bf16[6,6,4,512]{3,1,2,0:T(8,128)(2,1)S(1)}, bf16[6,6,4,512]{3,1,2,0:T(8,128)(2,1)S(1)}, u32[]{:S(2)}, u32[]{:S(2)}) collective-permute-start(bf16[6,6,4,512]{3,1,2,0:T(8,128)(2,1)S(1)} %get-tuple-element.26), channel_id=1, source_target_pairs={{0,31},{1,0},{2,1},{3,2},{4,3},{5,4},{6,5},{7,6},{8,7},{9,8},{10,9... | collective-permute-start | bytes 442376 | tf_op jit(solution)/shard_map/ppermute | solution.py:21
  34.5 2.9 %collective-permute-done = bf16[6,6,4,512]{3,1,2,0:T(8,128)(2,1)S(1)} collective-permute-done((bf16[6,6,4,512]{3,1,2,0:T(8,128)(2,1)S(1)}, bf16[6,6,4,512]{3,1,2,0:T(8,128)(2,1)S(1)}, u32[]{:S(2)}, u32[]{:S(2)}) %collective-permute-start) | collective-permute-done | bytes 147488 | tf_op jit(solution)/shard_map/ppermute | solution.py:21
  38.8 6.8 %collective-permute-done.1 = bf16[3,12,4,512]{3,1,2,0:T(8,128)(2,1)S(1)} collective-permute-done((bf16[3,12,4,512]{3,1,2,0:T(8,128)(2,1)S(1)}, bf16[3,12,4,512]{3,1,2,0:T(8,128)(2,1)S(1)}, u32[]{:S(2)}, u32[]{:S(2)}) %collective-permute-start.1) | collective-permute-done | bytes 147488 | tf_op jit(solution)/shard_map/ppermute | solution.py:21
  46.9 3.0 %convolution_convert_fusion = bf16[288,1536]{1,0:T(8,128)(2,1)} fusion(bf16[288,512]{1,0:T(8,128)(2,1)S(1)} %reshape_reshape.15, bf16[512,1536]{1,0:T(8,128)(2,1)} %param.17), kind=kOutput, calls=%fused_computation.11 | convolution fusion | flops 453427200 | bytes 2752512 | tf_op jit(solution)/shard_map/dot_general | solution.py:55
  49.8 1.6 %copy.60 = bf16[288,1536]{0,1:T(8,128)(2,1)S(1)} copy(bf16[288,1536]{1,0:T(8,128)(2,1)} %convolution_convert_fusion) | data formatting | bytes 1769472 | tf_op jit(solution)/shard_map/convert_element_type | solution.py:57
  51.5 1.5 %reshape.227 = bf16[2,144,3,16,32]{1,0,4,3,2:T(2,128)(2,1)} reshape(bf16[288,1536]{0,1:T(8,128)(2,1)S(1)} %copy.60) | data formatting | bytes 1769472 | tf_op jit(solution)/shard_map/reshape | solution.py:58
  53.0 3.7 %fusion.95 = (bf16[2,144,1,16,32]{1,0,4,3,2:T(2,128)(2,1)S(1)}, bf16[2,144,1,16,32]{1,0,4,3,2:T(2,128)(2,1)S(1)}, bf16[2,144,1,16,32]{1,0,4,3,2:T(2,128)(2,1)}) fusion(bf16[2,144,3,16,32]{1,0,4,3,2:T(2,128)(2,1)} %reshape.227), kind=kLoop, calls=%fused_computation.155 | loop fusion | bytes 1769472 | tf_op jit(solution)/shard_map/slice | solution.py:72
  56.7 5.1 %fusion.101 = (f32[2,16,144]{2,1,0:T(8,128)S(1)}, f32[2,16,144,144]{2,3,1,0:T(8,128)}) fusion(pred[2,144,144]{1,2,0:T(8,128)(4,1)S(1)} %broadcast_compare_fusion, bf16[2,144,1,16,32]{1,0,4,3,2:T(2,128)(2,1)S(1)} %get-tuple-element.16, bf16[2,144,1,16,32]{1,0,4,3,2:T(2,128)(2,1)} %get-tuple-element.17), kind=kOutput, calls=%fused_computation.161 | convolution fusion | flops 45121680 | bytes 3303936 | tf_op jit(solution)/shard_map/sub | solution.py:69
  61.8 3.6 %fusion.24 = bf16[2,144,16,32]{1,3,2,0:T(8,128)(2,1)} fusion(f32[2,16,144,144]{2,3,1,0:T(8,128)} %get-tuple-element.38, f32[2,16,144]{2,1,0:T(8,128)S(1)} %get-tuple-element.37, bf16[2,144,1,16,32]{1,0,4,3,2:T(2,128)(2,1)S(1)} %get-tuple-element.15), kind=kOutput, calls=%fused_computation.33 | convolution fusion | flops 43941888 | bytes 3262464 | tf_op jit(solution)/shard_map/whst,wthd->wshd/dot_general | solution.py:71
  65.4 1.9 %copy.65 = bf16[2,144,16,32]{3,2,1,0:T(8,128)(2,1)S(1)} copy(bf16[2,144,16,32]{1,3,2,0:T(8,128)(2,1)} %fusion.24) | data formatting | bytes 589824 | tf_op jit(solution)/shard_map/convert_element_type | solution.py:73
  67.3 1.6 %reshape_reshape.16 = bf16[1,1,2,6,12,2,512]{6,5,4,3,2,1,0:T(2,128)(2,1)} reshape(bf16[2,144,16,32]{3,2,1,0:T(8,128)(2,1)S(1)} %copy.65) | data formatting | bytes 589824 | tf_op jit(solution)/shard_map/reshape;reshape | solution.py:42
  70.1 1.4 %convolution_convert_fusion.2 = bf16[6,12,4,512]{3,1,2,0:T(8,128)(2,1)S(1)} fusion(bf16[512,512]{1,0:T(8,128)(2,1)} %param.18, bf16[6,12,3,512]{3,1,2,0:T(8,128)(2,1)S(1)} %slice.137, bf16[6,12,1,512]{3,1,2,0:T(8,128)(2,1)S(1)} %slice.136), kind=kOutput, calls=%fused_computation.31 | convolution fusion | flops 151289856 | bytes 1114112 | tf_op jit(solution)/shard_map/dot_general | solution.py:79
  71.6 5.7 %collective-permute-done.2 = bf16[3,12,4,512]{3,1,2,0:T(8,128)(2,1)S(1)} collective-permute-done((bf16[3,12,4,512]{3,1,2,0:T(8,128)(2,1)S(1)}, bf16[3,12,4,512]{3,1,2,0:T(8,128)(2,1)S(1)}, u32[]{:S(2)}, u32[]{:S(2)}) %collective-permute-start.2) | collective-permute-done | bytes 147488 | tf_op jit(solution)/shard_map/ppermute | solution.py:21
  77.7 8.7 %collective-permute-done.3 = bf16[6,6,4,512]{3,1,2,0:T(8,128)(2,1)S(1)} collective-permute-done((bf16[6,6,4,512]{3,1,2,0:T(8,128)(2,1)S(1)}, bf16[6,6,4,512]{3,1,2,0:T(8,128)(2,1)S(1)}, u32[]{:S(2)}, u32[]{:S(2)}) %collective-permute-start.3) | collective-permute-done | bytes 147488 | tf_op jit(solution)/shard_map/ppermute | solution.py:21
  87.5 4.0 %fusion.25 = f32[288,512]{1,0:T(8,128)} fusion(bf16[2048,512]{1,0:T(8,128)(2,1)S(1)} %copy-done, bf16[288,512]{1,0:T(8,128)(2,1)S(1)} %reshape.229, bf16[512,2048]{1,0:T(8,128)(2,1)} %param.20), kind=kOutput, calls=%fused_computation.39 | convolution fusion | flops 1213267968 | bytes 5079040 | tf_op jit(solution)/shard_map/dot_general | solution.py:165
  91.6 1.2 %reshape.230 = f32[6,12,4,512]{3,2,1,0:T(4,128)S(1)} reshape(f32[288,512]{1,0:T(8,128)} %fusion.25) | data formatting | bytes 1179648 | tf_op jit(solution)/shard_map/reshape | solution.py:165
  94.4 1.6 %fusion.33 = f32[72,1024]{1,0:T(8,128)S(1)} fusion(bf16[2048,1024]{1,0:T(8,128)(2,1)} %param.23, f32[72,512]{1,0:T(8,128)S(1)} %reshape.232, f32[512]{0:T(512)S(1)} %get-tuple-element.33, f32[72]{0:T(128)S(1)} %reshape.238, f32[72]{0:T(128)S(1)} %div.55), kind=kOutput, calls=%fused_computation.48 | convolution fusion | flops 75644928 | bytes 1493568 | tf_op jit(solution)/shard_map/dot_general | solution.py:112
  96.0 1.6 %convolution_add_fusion.3 = f32[72,1024]{1,0:T(8,128)S(1)} fusion(f32[72,1024]{1,0:T(8,128)S(1)} %fusion.33, bf16[2048,1024]{1,0:T(8,128)(2,1)} %param.23, f32[72,512]{1,0:T(8,128)S(1)} %reshape.235, f32[512]{0:T(512)S(1)} %get-tuple-element.32, f32[72]{0:T(128)S(1)} %reshape.238, f32[72]{0:T(128)S(1)} %div.55), kind=kOutput, calls=%fused_computation.42 | convolution fusion | flops 75718656 | bytes 1788480 | tf_op jit(solution)/shard_map/dot_general | solution.py:112
  97.6 1.6 %convolution_add_fusion.2 = f32[72,1024]{1,0:T(8,128)S(1)} fusion(f32[72,1024]{1,0:T(8,128)S(1)} %convolution_add_fusion.3, bf16[2048,1024]{1,0:T(8,128)(2,1)} %param.23, f32[72,512]{1,0:T(8,128)S(1)} %reshape.236, f32[512]{0:T(512)S(1)} %get-tuple-element.34, f32[72]{0:T(128)S(1)} %reshape.238, f32[72]{0:T(128)S(1)} %div.55), kind=kOutput, calls=%fused_computation.41 | convolution fusion | flops 75718656 | bytes 1788480 | tf_op jit(solution)/shard_map/dot_general | solution.py:112
  99.2 1.6 %fusion.27 = bf16[72,1024]{1,0:T(8,128)(2,1)S(1)} fusion(f32[72,1024]{1,0:T(8,128)S(1)} %convolution_add_fusion.2, bf16[2048,1024]{1,0:T(8,128)(2,1)} %param.23, f32[72,512]{1,0:T(8,128)S(1)} %reshape.237, f32[512]{0:T(512)S(1)} %get-tuple-element.31, f32[72]{0:T(128)S(1)} %reshape.238, f32[72]{0:T(128)S(1)} %div.55), kind=kOutput, calls=%fused_computation.43 | convolution fusion | flops 75792384 | bytes 1641024 | tf_op jit(solution)/shard_map/dot_general | solution.py:112
  (67 shorter events, 10.8 us)
Async XLA Ops:
  0.0 87.5 %copy-start = (bf16[2048,512]{1,0:T(8,128)(2,1)S(1)}, bf16[2048,512]{1,0:T(8,128)(2,1)}, u32[]{:S(2)}) copy-start(bf16[2048,512]{1,0:T(8,128)(2,1)} %param.21) | copy-start | bytes 6291460
  24.0 22.1 %copy-start.4 = (f32[512]{0:T(512)S(1)}, f32[512]{0:T(512)}, u32[]{:S(2)}) copy-start(f32[512]{0:T(512)} %param.16) | copy-start | bytes 6148
  25.5 0.7 copy-start.1
  26.3 11.2 %collective-permute-start = (bf16[6,6,4,512]{3,1,2,0:T(8,128)(2,1)S(1)}, bf16[6,6,4,512]{3,1,2,0:T(8,128)(2,1)S(1)}, u32[]{:S(2)}, u32[]{:S(2)}) collective-permute-start(bf16[6,6,4,512]{3,1,2,0:T(8,128)(2,1)S(1)} %get-tuple-element.26), channel_id=1, source_target_pairs={{0,31},{1,0},{2,1},{3,2},{4,3},{5,4},{6,5},{7,6},{8,7},{9,8},{10,9... | collective-permute-start | bytes 442376 | tf_op jit(solution)/shard_map/ppermute | solution.py:21
  37.6 8.0 %collective-permute-start.1 = (bf16[3,12,4,512]{3,1,2,0:T(8,128)(2,1)S(1)}, bf16[3,12,4,512]{3,1,2,0:T(8,128)(2,1)S(1)}, u32[]{:S(2)}, u32[]{:S(2)}) collective-permute-start(bf16[3,12,4,512]{3,1,2,0:T(8,128)(2,1)S(1)} %get-tuple-element.24), channel_id=1, source_target_pairs={{0,224},{32,0},{64,32},{96,64},{128,96},{160,128},{192,160},{224,1... | collective-permute-start | bytes 442376 | tf_op jit(solution)/shard_map/ppermute | solution.py:21
  68.9 8.7 %copy-start.3 = (f32[2048]{0:T(1024)S(1)}, f32[2048]{0:T(1024)}, u32[]{:S(2)}) copy-start(f32[2048]{0:T(1024)} %param.22) | copy-start | bytes 24580
  68.9 17.4 %copy-start.2 = (bf16[6,12,4,512]{3,1,2,0:T(8,128)(2,1)S(1)}, bf16[6,12,4,512]{3,1,2,0:T(8,128)(2,1)}, u32[]{:S(2)}) copy-start(bf16[6,12,4,512]{3,1,2,0:T(8,128)(2,1)} %copy-done.1) | copy-start | bytes 884740
  70.0 16.9 %copy-start.5 = (f32[512]{0:T(512)S(1)}, f32[512]{0:T(512)}, u32[]{:S(2)}) copy-start(f32[512]{0:T(512)} %param.19) | copy-start | bytes 6148
  71.5 5.7 %collective-permute-start.2 = (bf16[3,12,4,512]{3,1,2,0:T(8,128)(2,1)S(1)}, bf16[3,12,4,512]{3,1,2,0:T(8,128)(2,1)S(1)}, u32[]{:S(2)}, u32[]{:S(2)}) collective-permute-start(bf16[3,12,4,512]{3,1,2,0:T(8,128)(2,1)S(1)} %get-tuple-element.21), channel_id=1, source_target_pairs={{0,32},{32,64},{64,96},{96,128},{128,160},{160,192},{192,224},{224... | collective-permute-start | bytes 442376 | tf_op jit(solution)/shard_map/ppermute | solution.py:21
  77.4 9.0 %collective-permute-start.3 = (bf16[6,6,4,512]{3,1,2,0:T(8,128)(2,1)S(1)}, bf16[6,6,4,512]{3,1,2,0:T(8,128)(2,1)S(1)}, u32[]{:S(2)}, u32[]{:S(2)}) collective-permute-start(bf16[6,6,4,512]{3,1,2,0:T(8,128)(2,1)S(1)} %fusion.59), channel_id=1, source_target_pairs={{0,1},{1,2},{2,3},{3,4},{4,5},{5,6},{6,7},{7,8},{8,9},{9,10},{10,1... | collective-permute-start | bytes 442376 | tf_op jit(solution)/shard_map/ppermute | solution.py:21
where the time goes:
time: 103 us; the launch traced here: 101 us
  matrix products  30 us (29%)
  local copies, waits for them, and re-layouts  26.5 us (26%)
  waiting for transfers between devices  24.1 us (23%)
  other arithmetic  11 us (11%)
  starting transfers between devices  9.47 us (9%)
    ppermute x4, waiting for transfers between devices, passed_along(): return lax.ppermute(value, axis, pairs)  24.1 us
    ppermute x4, starting transfers between devices, passed_along(): return lax.ppermute(value, axis, pairs)  9.47 us
    dot_general x4, matrix products, merge_patches(): jnp.dot(normed.reshape(-1, channels), weight[index * channels:(index + 1)...  6.33 us
    slice x2, local copies, waits for them, and re-layouts, window_attention(): projected[:, :, 2]  6.27 us
    dot_general x2, matrix products, window_attention(): jnp.dot(windows.reshape(win_count * win_size, width), w_qkv, preferred_el...  5.92 us
    sub x1, matrix products, window_attention(): weights = jnp.exp(scores - row_max)  5.08 us
    dot_general x2, matrix products, window_attention(): jnp.einsum('whst,wthd->wshd', probabilities, projected[:, :, 2], preferre...  4.84 us
    sub x1, other arithmetic, window_attention(): weights = jnp.exp(scores - row_max)  4.52 us
  transfers between devices with their start and end apart: 4, of which 4 were waited for; matrix products, arithmetic and copies ran while one was open for 0% of the time, Pallas kernels for 0%

commit v1 on v0

v1 whole, which is shorter than its diff:
```python
import functools
import math

import jax
import jax.numpy as jnp
import numpy as np
from jax import lax
from jax.experimental import pallas as pl
from jax.experimental.pallas import tpu as pltpu
from jax.sharding import PartitionSpec as P

HEADS = 16
HEAD = 32
WLAT = 6
WLON = 12
WLEV = 2
LEV = 4
HALF_LAT = WLAT // 2
HALF_LON = WLON // 2
WIN = WLAT * WLON * WLEV
TOKENS = WLAT * WLON * LEV
QUAD = TOKENS // 4
GROUP = 8
LANES = GROUP * HEAD

epsilon = 1e-05


def _quadrant_tokens():
    return [
        (half_r * HALF_LAT + r, half_c * HALF_LON + c, l)
        for half_r in range(2)
        for half_c in range(2)
        for l in range(LEV)
        for r in range(HALF_LAT)
        for c in range(HALF_LON)
    ]


def _window_tokens(level_order):
    return [
        (r, c, l) for l in level_order for r in range(WLAT) for c in range(WLON)
    ]


def _permutation(target, source):
    place = {token: index for index, token in enumerate(source)}
    matrix = np.zeros((len(target), len(source)), np.float32)
    for index, token in enumerate(target):
        matrix[index, place[token]] = 1.0
    return jnp.asarray(matrix, jnp.bfloat16)


def _natural_tokens():
    return [(r, c, l) for r in range(WLAT) for c in range(WLON) for l in range(LEV)]


def _merge_tokens():
    return [
        (2 * i + piece % 2, 2 * j + piece // 2, l)
        for piece in range(4)
        for i in range(WLAT // 2)
        for j in range(WLON // 2)
        for l in range(LEV)
    ]


def normed(values, gain_row):
    centered = values - jnp.mean(values, axis=-1, keepdims=True)
    spread = jnp.mean(centered * centered, axis=-1, keepdims=True)
    return centered * lax.rsqrt(spread + epsilon) * gain_row


def permuted(matrix, values):
    return jnp.dot(matrix, values, preferred_element_type=jnp.float32).astype(jnp.bfloat16)


def attention(tokens, w_qkv, w_out, allowed):
    width = tokens.shape[-1]
    scale = math.log2(math.e) / math.sqrt(HEAD)
    query = jnp.dot(tokens, w_qkv[:, :width], preferred_element_type=jnp.float32).astype(
        jnp.bfloat16
    )
    key = jnp.dot(
        tokens, w_qkv[:, width : 2 * width], preferred_element_type=jnp.float32
    ).astype(jnp.bfloat16)
    value = jnp.dot(
        tokens, w_qkv[:, 2 * width :], preferred_element_type=jnp.float32
    ).astype(jnp.bfloat16)
    lane = lax.broadcasted_iota(jnp.int32, (WIN, LANES), 1)
    masks = [
        ((lane >= h * HEAD) & (lane < (h + 1) * HEAD)).astype(jnp.float32).astype(jnp.bfloat16)
        for h in range(GROUP)
    ]
    contexts = []
    for w in range(TOKENS // WIN):
        parts = []
        for g in range(HEADS // GROUP):
            rows = slice(w * WIN, (w + 1) * WIN)
            cols = slice(g * LANES, (g + 1) * LANES)
            q, k, v = query[rows, cols], key[rows, cols], value[rows, cols]
            stacked = jnp.concatenate([q * m for m in masks], axis=0)
            scores = lax.dot_general(
                k, stacked, (((1,), (1,)), ((), ())), preferred_element_type=jnp.float32
            )
            if allowed is not None:
                scores = jnp.where(allowed(w), scores, jnp.float32(-1e30))
            weights = jnp.exp2((scores - jnp.max(scores, axis=0, keepdims=True)) * scale)
            probs = (weights * (1.0 / jnp.sum(weights, axis=0, keepdims=True))).astype(
                jnp.bfloat16
            )
            mixed = lax.dot_general(
                probs, v, (((0,), (0,)), ((), ())), preferred_element_type=jnp.float32
            )
            context = mixed[:WIN]
            for h in range(1, GROUP):
                context = jnp.where(lane >= h * HEAD, mixed[h * WIN : (h + 1) * WIN], context)
            parts.append(context.astype(jnp.bfloat16))
        contexts.append(jnp.concatenate(parts, axis=1))
    context = jnp.concatenate(contexts, axis=0)
    return jnp.dot(context, w_out, preferred_element_type=jnp.float32)


def window_kernel(x_ref, to_win_ref, to_quad_ref, gain_ref, w_qkv_ref, w_out_ref, *outs):
    x = x_ref[...].astype(jnp.float32).reshape(TOKENS, x_ref.shape[-1]).astype(jnp.bfloat16)
    x = jnp.dot(to_win_ref[...], x, preferred_element_type=jnp.float32)
    tokens = normed(x, gain_ref[...]).astype(jnp.bfloat16)
    after = (x + attention(tokens, w_qkv_ref[...], w_out_ref[...], None)).astype(jnp.bfloat16)
    after = jnp.dot(to_quad_ref[...], after, preferred_element_type=jnp.float32)
    for index, out in enumerate(outs):
        out[...] = after[index * QUAD : (index + 1) * QUAD].astype(jnp.bfloat16)


def shift_kernel(
    last_ref, a_ref, b_ref, c_ref, d_ref, to_win_ref, to_quad_ref, gain_ref, w_qkv_ref, w_out_ref, *outs
):
    x = jnp.concatenate(
        [ref[...].astype(jnp.float32) for ref in (a_ref, b_ref, c_ref, d_ref)], axis=0
    )
    tokens = normed(x, gain_ref[...]).astype(jnp.bfloat16)
    tokens = permuted(to_win_ref[...], tokens)
    last = last_ref[0, 0]
    half = WIN // WLEV

    def code(position, w):
        level = (position >= half).astype(jnp.int32) if w == 1 else 0
        southern = (lax.rem(position, half) >= half // 2).astype(jnp.int32)
        return level + 2 * last * southern

    def allowed(w):
        shape = (WIN, GROUP * WIN)
        of_key = code(lax.broadcasted_iota(jnp.int32, shape, 0), w)
        of_query = code(lax.rem(lax.broadcasted_iota(jnp.int32, shape, 1), WIN), w)
        return of_key == of_query

    branch = attention(tokens, w_qkv_ref[...], w_out_ref[...], allowed).astype(jnp.bfloat16)
    branch = jnp.dot(to_quad_ref[...], branch, preferred_element_type=jnp.float32)
    for index, out in enumerate(outs):
        out[...] = branch[index * QUAD : (index + 1) * QUAD].astype(jnp.bfloat16)


def merge_kernel(
    a0, a1, a2, a3, b0, b1, b2, b3, to_merge_ref, gain_mlp_ref, w_up_ref, w_down_ref, gain_merge_ref, w_merge_ref, out_ref
):
    after = jnp.concatenate([ref[...].astype(jnp.float32) for ref in (a0, a1, a2, a3)], axis=0)
    branch = jnp.concatenate([ref[...].astype(jnp.float32) for ref in (b0, b1, b2, b3)], axis=0)
    shift = (after + branch).astype(jnp.bfloat16).astype(jnp.float32)
    tokens = normed(shift, gain_mlp_ref[...]).astype(jnp.bfloat16)
    hidden = jax.nn.gelu(
        jnp.dot(tokens, w_up_ref[...], preferred_element_type=jnp.float32), approximate=True
    ).astype(jnp.bfloat16)
    after_mlp = (
        shift + jnp.dot(hidden, w_down_ref[...], preferred_element_type=jnp.float32)
    ).astype(jnp.bfloat16)
    pieces = jnp.dot(to_merge_ref[...], after_mlp, preferred_element_type=jnp.float32)
    stacked = jnp.concatenate(
        [pieces[index * QUAD : (index + 1) * QUAD] for index in range(4)], axis=1
    )
    tokens = normed(stacked, gain_merge_ref[...]).astype(jnp.bfloat16)
    merged = jnp.dot(tokens, w_merge_ref[...], preferred_element_type=jnp.float32)
    out_ref[...] = merged.reshape(out_ref.shape).astype(jnp.bfloat16)


def _call(kernel, operands, out_shape, smem=()):
    return pl.pallas_call(
        kernel,
        out_shape=out_shape,
        in_specs=[
            pl.BlockSpec(memory_space=pltpu.SMEM if index in smem else pltpu.VMEM)
            for index in range(len(operands))
        ],
        out_specs=jax.tree.map(lambda _: pl.BlockSpec(memory_space=pltpu.VMEM), out_shape),
        compiler_params=pltpu.CompilerParams(vmem_limit_bytes=56 * 1024 * 1024),
    )(*operands)


def _fetched(value, rows, cols):
    lats, lons = lax.axis_size("lat"), lax.axis_size("lon")
    if not rows:
        return lax.ppermute(value, "lon", [((j + cols) % lons, j) for j in range(lons)])
    if not cols:
        return lax.ppermute(value, "lat", [((i + rows) % lats, i) for i in range(lats)])
    pairs = [
        (((i + rows) % lats) * lons + (j + cols) % lons, i * lons + j)
        for i in range(lats)
        for j in range(lons)
    ]
    return lax.ppermute(value, ("lat", "lon"), pairs)


def on_device(
    latent_field, gain_win, w_qkv_win, w_out_win, gain_shift, w_qkv_shift, w_out_shift,
    gain_mlp, w_up, w_down, gain_merge, w_merge,
):
    width = latent_field.shape[-1]
    quad = jax.ShapeDtypeStruct((QUAD, width), jnp.bfloat16)
    quads = _quadrant_tokens()
    plain = _window_tokens((0, 1, 2, 3))
    rolled = _window_tokens((1, 2, 3, 0))
    last = (lax.axis_index("lat") == lax.axis_size("lat") - 1).astype(jnp.int32).reshape(1, 1)

    x = latent_field.reshape(WLAT * WLON, LEV, width)
    nw, ne, sw, se = _call(
        window_kernel,
        (
            x, _permutation(plain, _natural_tokens()), _permutation(quads, plain),
            gain_win.reshape(1, -1), w_qkv_win, w_out_win,
        ),
        (quad,) * 4,
    )
    east = _fetched(sw, 0, 1)
    south = _fetched(ne, 1, 0)
    corner = _fetched(nw, 1, 1)
    own, to_east, to_south, to_corner = _call(
        shift_kernel,
        (
            last, se, east, south, corner, _permutation(rolled, quads),
            _permutation(quads, rolled), gain_shift.reshape(1, -1), w_qkv_shift, w_out_shift,
        ),
        (quad,) * 4,
        smem=(0,),
    )
    b_sw = _fetched(to_east, 0, -1)
    b_ne = _fetched(to_south, -1, 0)
    b_nw = _fetched(to_corner, -1, -1)
    merged = _call(
        merge_kernel,
        (
            nw, ne, sw, se, b_nw, b_ne, b_sw, own, _permutation(_merge_tokens(), quads),
            gain_mlp.reshape(1, -1), w_up, w_down, gain_merge.reshape(1, -1), w_merge,
        ),
        jax.ShapeDtypeStruct((QUAD // LEV, LEV, 2 * width), jnp.bfloat16),
    )
    return merged.reshape(WLAT // 2, WLON // 2, LEV, 2 * width)


def solution(mesh):
    in_specs = (P("lat", "lon", None, None),) + (P(),) * 11
    return jax.shard_map(
        on_device,
        mesh=mesh,
        in_specs=in_specs,
        out_specs=P("lat", "lon", None, None),
        check_vma=False,
    )
```

time: 103 us -> 44.8 us (0.43)
  matrix products: 30 us -> 0 us
  local copies, waits for them, and re-layouts: 26.5 us -> 1.31 us
  Pallas kernels: 0 us -> 19 us
  other arithmetic: 11 us -> 0 us
  waiting for transfers between devices: 24.1 us -> 14.5 us
    dot_general x12 -> x0, matrix products: 24.9 us -> none  [the longest x4 6.33 us: merge_patches(): jnp.dot(normed.reshape(-1, channels), weight[index * channels:(index + 1)...]
    pallas_call x0 -> x3, Pallas kernels: none -> 19 us  [_call(): pl.pallas_call(kernel, out_shape=out_shape, in_specs=[pl.BlockSpec(memory...]
    ppermute x4 -> x6, waiting for transfers between devices: 24.1 us -> 14.5 us  [the longest x2 10.1 us: _fetched(): return lax.ppermute(value, ('lat', 'lon'), pairs)]
    convert_element_type x11 -> x0, local copies, waits for them, and re-layouts: 8.57 us -> none  [the longest x2 3.87 us: window_attention(): context = jnp.einsum('whst,wthd->wshd', probabilities, projected[:, :, 2]...]
    slice x9 -> x0, local copies, waits for them, and re-layouts: 6.43 us -> none  [the longest x2 6.27 us: window_attention(): projected[:, :, 2]]
    sub x1 -> x0, matrix products: 5.08 us -> none  [window_attention(): weights = jnp.exp(scores - row_max)]
    reshape x6 -> x0, local copies, waits for them, and re-layouts: 4.88 us -> none  [the longest x2 2.97 us: window_attention(): projected = projected.reshape(win_count, win_size, 3, HEADS, HEAD)]
    sub x1 -> x0, other arithmetic: 4.52 us -> none  [window_attention(): weights = jnp.exp(scores - row_max)]
  transfers between devices with their start and end apart: 4 -> 6, of which waited for: 4 -> 3; matrix products, arithmetic and copies ran while one was open for 0% -> 0% of each run, Pallas kernels for 0% -> 0%
where the time goes in v1:
time: 44.8 us; the launch traced here: 44.3 us
  Pallas kernels  19 us (42%)
  waiting for transfers between devices  14.5 us (32%)
  starting transfers between devices  9.43 us (21%)
  local copies, waits for them, and re-layouts  1.31 us (3%)
    pallas_call x3, Pallas kernels, _call(): pl.pallas_call(kernel, out_shape=out_shape, in_specs=[pl.BlockSpec(memory...  19 us
    ppermute x2, waiting for transfers between devices, _fetched(): return lax.ppermute(value, ('lat', 'lon'), pairs)  10.1 us
    ppermute x2, starting transfers between devices, _fetched(): return lax.ppermute(value, ('lat', 'lon'), pairs)  8.2 us
    ppermute x2, waiting for transfers between devices, _fetched(): lax.ppermute(value, 'lat', [((i + rows) % lats, i) for i in range(lats)])  4.37 us
    unnamed x12, local copies, waits for them, and re-layouts  1.31 us
  transfers between devices with their start and end apart: 6, of which 3 were waited for; matrix products, arithmetic and copies ran while one was open for 0% of the time, Pallas kernels for 0%

profile of v1, /device:TPU:6, one launch (start us, length us, event | category | flops | bytes accessed | tf_op | source)
XLA Modules:
  0.0 44.3 jit_solution(7869634710530512794)
XLA Ops:
  0.0 5.7 %shard_map.163 = (bf16[72,512]{1,0:T(8,128)(2,1)}, bf16[72,512]{1,0:T(8,128)(2,1)}, bf16[72,512]{1,0:T(8,128)(2,1)}, bf16[72,512]{1,0:T(8,128)(2,1)}) custom-call(bf16[72,4,512]{2,1,0:T(4,128)(2,1)} %bitcast.7, bf16[288,288]{1,0:T(8,128)(2,1)} %constant.18.clone.to_win_ref, bf16[288,288]{1,0:T(8,128)(2,1)} %constant.19.clone.to_quad_ref, f32[1,512]{1,0:T(1,128)} %bitcast.9, ...), custom_call_target="tpu_custom_call" | custom-call | tf_op jit(solution)/shard_map/pallas_call | solution.py:185
  5.7 8.2 %collective-permute-start.2 = (bf16[72,512]{1,0:T(8,128)(2,1)}, bf16[72,512]{1,0:T(8,128)(2,1)S(1)}, u32[]{:S(2)}, u32[]{:S(2)}) collective-permute-start(bf16[72,512]{1,0:T(8,128)(2,1)} %get-tuple-element.13.a0), channel_id=1, source_target_pairs={{33,0},{34,1},{35,2},{36,3},{37,4},{38,5},{39,6},{40,7},{41,8},{42... | collective-permute-start | bytes 221192 | tf_op jit(solution)/shard_map/ppermute | solution.py:208
  13.9 0.5 %collective-permute-start.1 = (bf16[72,512]{1,0:T(8,128)(2,1)}, bf16[72,512]{1,0:T(8,128)(2,1)S(1)}, u32[]{:S(2)}, u32[]{:S(2)}) collective-permute-start(bf16[72,512]{1,0:T(8,128)(2,1)} %get-tuple-element.14.a1), channel_id=1, source_target_pairs={{32,0},{64,32},{96,64},{128,96},{160,128},{192,160},{224,192},{0,2... | collective-permute-start | bytes 221192 | tf_op jit(solution)/shard_map/ppermute | solution.py:202
  14.5 0.6 %collective-permute-start = (bf16[72,512]{1,0:T(8,128)(2,1)}, bf16[72,512]{1,0:T(8,128)(2,1)S(1)}, u32[]{:S(2)}, u32[]{:S(2)}) collective-permute-start(bf16[72,512]{1,0:T(8,128)(2,1)} %get-tuple-element.15.a2), channel_id=1, source_target_pairs={{1,0},{2,1},{3,2},{4,3},{5,4},{6,5},{7,6},{8,7},{9,8},{10,9},{11,1... | collective-permute-start | bytes 221192 | tf_op jit(solution)/shard_map/ppermute | solution.py:200
  15.0 1.2 %collective-permute-done.2.d_ref = bf16[72,512]{1,0:T(8,128)(2,1)S(1)} collective-permute-done((bf16[72,512]{1,0:T(8,128)(2,1)}, bf16[72,512]{1,0:T(8,128)(2,1)S(1)}, u32[]{:S(2)}, u32[]{:S(2)}) %collective-permute-start.2) | collective-permute-done | bytes 73760 | tf_op jit(solution)/shard_map/ppermute | solution.py:208
  16.2 0.0 copy-start.3
  16.2 4.4 %collective-permute-done.1.c_ref = bf16[72,512]{1,0:T(8,128)(2,1)S(1)} collective-permute-done((bf16[72,512]{1,0:T(8,128)(2,1)}, bf16[72,512]{1,0:T(8,128)(2,1)S(1)}, u32[]{:S(2)}, u32[]{:S(2)}) %collective-permute-start.1) | collective-permute-done | bytes 73760 | tf_op jit(solution)/shard_map/ppermute | solution.py:202
  20.6 0.0 copy-start.4
  20.6 0.0 collective-permute-done.b_ref
  20.6 0.0 copy-start.5
  20.6 0.0 copy-done.3
  20.6 0.6 %copy-done.4 = bf16[72,512]{1,0:T(8,128)(2,1)} copy-done((bf16[72,512]{1,0:T(8,128)(2,1)}, bf16[72,512]{1,0:T(8,128)(2,1)S(1)}, u32[]{:S(2)}) %copy-start.4) | copy-done | bytes 73752
  21.2 0.0 copy-done.5
  21.3 5.8 %shard_map.164 = (bf16[72,512]{1,0:T(8,128)(2,1)}, bf16[72,512]{1,0:T(8,128)(2,1)}, bf16[72,512]{1,0:T(8,128)(2,1)}, bf16[72,512]{1,0:T(8,128)(2,1)}) custom-call(s32[1,1]{1,0:T(1,128)} %bitcast.2.last_ref, bf16[72,512]{1,0:T(8,128)(2,1)} %get-tuple-element.16.a_ref.a3, bf16[72,512]{1,0:T(8,128)(2,1)} %copy-done.5, bf16[72,512]{1,0:T(8,128)(2,1)} %copy-done.4, ...), custom_call_target="tpu_custom_call" | custom-call | tf_op jit(solution)/shard_map/pallas_call | solution.py:185
  27.1 0.0 collective-permute-start.3
  27.1 0.1 collective-permute-start.4
  27.1 0.1 collective-permute-start.5
  27.2 8.9 %collective-permute-done.3.b0 = bf16[72,512]{1,0:T(8,128)(2,1)S(1)} collective-permute-done((bf16[72,512]{1,0:T(8,128)(2,1)}, bf16[72,512]{1,0:T(8,128)(2,1)S(1)}, u32[]{:S(2)}, u32[]{:S(2)}) %collective-permute-start.3) | collective-permute-done | bytes 73760 | tf_op jit(solution)/shard_map/ppermute | solution.py:208
  36.1 0.0 copy-start
  36.1 0.0 collective-permute-done.4.b1
  36.1 0.0 copy-start.1
  36.1 0.0 collective-permute-done.5.b2
  36.1 0.0 copy-start.2
  36.2 0.6 %copy-done = bf16[72,512]{1,0:T(8,128)(2,1)} copy-done((bf16[72,512]{1,0:T(8,128)(2,1)}, bf16[72,512]{1,0:T(8,128)(2,1)S(1)}, u32[]{:S(2)}) %copy-start) | copy-done | bytes 73752
  36.8 0.0 copy-done.1
  36.8 0.0 copy-done.2
  36.8 7.5 %shard_map.165 = bf16[18,4,1024]{2,1,0:T(4,128)(2,1)} custom-call(bf16[72,512]{1,0:T(8,128)(2,1)} %get-tuple-element.13.a0, bf16[72,512]{1,0:T(8,128)(2,1)} %get-tuple-element.14.a1, bf16[72,512]{1,0:T(8,128)(2,1)} %get-tuple-element.15.a2, bf16[72,512]{1,0:T(8,128)(2,1)} %get-tuple-element.16.a_ref.a3, bf16[72,512]{1,0:T(8,128)(2,1)} %copy-done, ...), custom_call_target="tpu_custom_call" | custom-call | tf_op jit(solution)/shard_map/pallas_call | solution.py:185
Async XLA Ops:
  5.7 10.5 %collective-permute-start.2 = (bf16[72,512]{1,0:T(8,128)(2,1)}, bf16[72,512]{1,0:T(8,128)(2,1)S(1)}, u32[]{:S(2)}, u32[]{:S(2)}) collective-permute-start(bf16[72,512]{1,0:T(8,128)(2,1)} %get-tuple-element.13.a0), channel_id=1, source_target_pairs={{33,0},{34,1},{35,2},{36,3},{37,4},{38,5},{39,6},{40,7},{41,8},{42... | collective-permute-start | bytes 221192 | tf_op jit(solution)/shard_map/ppermute | solution.py:208
  13.9 6.7 %collective-permute-start.1 = (bf16[72,512]{1,0:T(8,128)(2,1)}, bf16[72,512]{1,0:T(8,128)(2,1)S(1)}, u32[]{:S(2)}, u32[]{:S(2)}) collective-permute-start(bf16[72,512]{1,0:T(8,128)(2,1)} %get-tuple-element.14.a1), channel_id=1, source_target_pairs={{32,0},{64,32},{96,64},{128,96},{160,128},{192,160},{224,192},{0,2... | collective-permute-start | bytes 221192 | tf_op jit(solution)/shard_map/ppermute | solution.py:202
  14.5 6.1 %collective-permute-start = (bf16[72,512]{1,0:T(8,128)(2,1)}, bf16[72,512]{1,0:T(8,128)(2,1)S(1)}, u32[]{:S(2)}, u32[]{:S(2)}) collective-permute-start(bf16[72,512]{1,0:T(8,128)(2,1)} %get-tuple-element.15.a2), channel_id=1, source_target_pairs={{1,0},{2,1},{3,2},{4,3},{5,4},{6,5},{7,6},{8,7},{9,8},{10,9},{11,1... | collective-permute-start | bytes 221192 | tf_op jit(solution)/shard_map/ppermute | solution.py:200
  16.2 4.4 %copy-start.3 = (bf16[72,512]{1,0:T(8,128)(2,1)}, bf16[72,512]{1,0:T(8,128)(2,1)S(1)}, u32[]{:S(2)}) copy-start(bf16[72,512]{1,0:T(8,128)(2,1)S(1)} %collective-permute-done.2.d_ref) | copy-start | bytes 221188
  20.6 0.6 %copy-start.4 = (bf16[72,512]{1,0:T(8,128)(2,1)}, bf16[72,512]{1,0:T(8,128)(2,1)S(1)}, u32[]{:S(2)}) copy-start(bf16[72,512]{1,0:T(8,128)(2,1)S(1)} %collective-permute-done.1.c_ref) | copy-start | bytes 221188
  20.6 0.7 %copy-start.5 = (bf16[72,512]{1,0:T(8,128)(2,1)}, bf16[72,512]{1,0:T(8,128)(2,1)S(1)}, u32[]{:S(2)}) copy-start(bf16[72,512]{1,0:T(8,128)(2,1)S(1)} %collective-permute-done.b_ref) | copy-start | bytes 221188
  27.1 9.0 %collective-permute-start.3 = (bf16[72,512]{1,0:T(8,128)(2,1)}, bf16[72,512]{1,0:T(8,128)(2,1)S(1)}, u32[]{:S(2)}, u32[]{:S(2)}) collective-permute-start(bf16[72,512]{1,0:T(8,128)(2,1)} %get-tuple-element.17), channel_id=1, source_target_pairs={{255,0},{224,1},{225,2},{226,3},{227,4},{228,5},{229,6},{230,7},{2... | collective-permute-start | bytes 221192 | tf_op jit(solution)/shard_map/ppermute | solution.py:208
  27.1 9.1 %collective-permute-start.4 = (bf16[72,512]{1,0:T(8,128)(2,1)}, bf16[72,512]{1,0:T(8,128)(2,1)S(1)}, u32[]{:S(2)}, u32[]{:S(2)}) collective-permute-start(bf16[72,512]{1,0:T(8,128)(2,1)} %get-tuple-element.18), channel_id=1, source_target_pairs={{224,0},{0,32},{32,64},{64,96},{96,128},{128,160},{160,192},{192,2... | collective-permute-start | bytes 221192 | tf_op jit(solution)/shard_map/ppermute | solution.py:202
  27.1 9.0 %collective-permute-start.5 = (bf16[72,512]{1,0:T(8,128)(2,1)}, bf16[72,512]{1,0:T(8,128)(2,1)S(1)}, u32[]{:S(2)}, u32[]{:S(2)}) collective-permute-start(bf16[72,512]{1,0:T(8,128)(2,1)} %get-tuple-element.19), channel_id=1, source_target_pairs={{31,0},{0,1},{1,2},{2,3},{3,4},{4,5},{5,6},{6,7},{7,8},{8,9},{9,10... | collective-permute-start | bytes 221192 | tf_op jit(solution)/shard_map/ppermute | solution.py:200
  36.1 0.6 %copy-start = (bf16[72,512]{1,0:T(8,128)(2,1)}, bf16[72,512]{1,0:T(8,128)(2,1)S(1)}, u32[]{:S(2)}) copy-start(bf16[72,512]{1,0:T(8,128)(2,1)S(1)} %collective-permute-done.3.b0) | copy-start | bytes 221188
  36.1 0.7 %copy-start.1 = (bf16[72,512]{1,0:T(8,128)(2,1)}, bf16[72,512]{1,0:T(8,128)(2,1)S(1)}, u32[]{:S(2)}) copy-start(bf16[72,512]{1,0:T(8,128)(2,1)S(1)} %collective-permute-done.4.b1) | copy-start | bytes 221188
  36.1 0.7 %copy-start.2 = (bf16[72,512]{1,0:T(8,128)(2,1)}, bf16[72,512]{1,0:T(8,128)(2,1)S(1)}, u32[]{:S(2)}) copy-start(bf16[72,512]{1,0:T(8,128)(2,1)S(1)} %collective-permute-done.5.b2) | copy-start | bytes 221188

commit v2 on v1

--- a/solution.py
+++ b/solution.py
@@ -22,6 +22,7 @@
 QUAD = TOKENS // 4
 GROUP = 8
 LANES = GROUP * HEAD
+VMEM_BYTES = 16 * 1024 * 1024
 
 epsilon = 1e-05
 
@@ -121,7 +122,20 @@
     return jnp.dot(context, w_out, preferred_element_type=jnp.float32)
 
 
-def window_kernel(x_ref, to_win_ref, to_quad_ref, gain_ref, w_qkv_ref, w_out_ref, *outs):
+def window_kernel(
+    x_hbm, to_win_hbm, to_quad_hbm, gain_hbm, w_qkv_hbm, w_out_hbm, *refs
+):
+    outs, held, sems = refs[:4], refs[4:-1], refs[-1]
+    sources = (x_hbm, to_win_hbm, gain_hbm, w_qkv_hbm, w_out_hbm, to_quad_hbm)
+    copies = [
+        pltpu.make_async_copy(source, target, sems.at[index])
+        for index, (source, target) in enumerate(zip(sources, held))
+    ]
+    for copy in copies:
+        copy.start()
+    x_ref, to_win_ref, gain_ref, w_qkv_ref, w_out_ref, to_quad_ref = held
+    for copy in copies:
+        copy.wait()
     x = x_ref[...].astype(jnp.float32).reshape(TOKENS, x_ref.shape[-1]).astype(jnp.bfloat16)
     x = jnp.dot(to_win_ref[...], x, preferred_element_type=jnp.float32)
     tokens = normed(x, gain_ref[...]).astype(jnp.bfloat16)
@@ -181,6 +195,35 @@
     out_ref[...] = merged.reshape(out_ref.shape).astype(jnp.bfloat16)
 
 
+def _in_hbm(array):
+    return pltpu.with_memory_space_constraint(array, pltpu.HBM)
+
+
+def prefetch_kernel(*refs):
+    count = (len(refs) - 2) // 2
+    sources, targets, sems = refs[1 : 1 + count], refs[1 + count : -1], refs[-1]
+    copies = [
+        pltpu.make_async_copy(source, target, sems.at[index])
+        for index, (source, target) in enumerate(zip(sources, targets))
+    ]
+    for copy in copies:
+        copy.start()
+    for copy in copies:
+        copy.wait()
+
+
+def _prefetched(after, arrays):
+    return pl.pallas_call(
+        prefetch_kernel,
+        out_shape=[pltpu.VMEM(array.shape, array.dtype) for array in arrays],
+        in_specs=[pl.BlockSpec(memory_space=pl.ANY)] + [pl.BlockSpec(memory_space=pltpu.HBM)] * len(arrays),
+        out_specs=[pl.BlockSpec(memory_space=pltpu.VMEM)] * len(arrays),
+        scratch_shapes=[pltpu.SemaphoreType.DMA((len(arrays),))],
+        compiler_params=pltpu.CompilerParams(vmem_limit_bytes=VMEM_BYTES),
+        cost_estimate=pl.CostEstimate(flops=0, bytes_accessed=24 * 1024 * 1024, transcendentals=0),
+    )(after, *map(_in_hbm, arrays))
+
+
 def _call(kernel, operands, out_shape, smem=()):
     return pl.pallas_call(
         kernel,
@@ -190,7 +233,7 @@
             for index in range(len(operands))
         ],
         out_specs=jax.tree.map(lambda _: pl.BlockSpec(memory_space=pltpu.VMEM), out_shape),
-        compiler_params=pltpu.CompilerParams(vmem_limit_bytes=56 * 1024 * 1024),
+        compiler_params=pltpu.CompilerParams(vmem_limit_bytes=VMEM_BYTES),
     )(*operands)
 
 
@@ -220,13 +263,28 @@
     last = (lax.axis_index("lat") == lax.axis_size("lat") - 1).astype(jnp.int32).reshape(1, 1)
 
     x = latent_field.reshape(WLAT * WLON, LEV, width)
-    nw, ne, sw, se = _call(
+    to_win, to_quad = _permutation(plain, _natural_tokens()), _permutation(quads, plain)
+    operands = (x, to_win, to_quad, gain_win.reshape(1, -1), w_qkv_win, w_out_win)
+    held = (x, to_win, gain_win.reshape(1, -1), w_qkv_win, w_out_win, to_quad)
+    nw, ne, sw, se = pl.pallas_call(
         window_kernel,
+        out_shape=(quad,) * 4,
+        in_specs=[pl.BlockSpec(memory_space=pltpu.HBM)] * len(operands),
+        out_specs=(pl.BlockSpec(memory_space=pltpu.VMEM),) * 4,
+        scratch_shapes=[pltpu.VMEM(array.shape, array.dtype) for array in held]
+        + [pltpu.SemaphoreType.DMA((len(held),))],
+        compiler_params=pltpu.CompilerParams(vmem_limit_bytes=VMEM_BYTES),
+    )(*map(_in_hbm, operands))
+    (
+        shift_in, shift_out, to_merge, gain_shift, w_qkv_shift, w_out_shift,
+        gain_mlp, w_up, w_down, gain_merge, w_merge,
+    ) = _prefetched(
+        nw,
         (
-            x, _permutation(plain, _natural_tokens()), _permutation(quads, plain),
-            gain_win.reshape(1, -1), w_qkv_win, w_out_win,
+            _permutation(rolled, quads), _permutation(quads, rolled),
+            _permutation(_merge_tokens(), quads), gain_shift.reshape(1, -1), w_qkv_shift,
+            w_out_shift, gain_mlp.reshape(1, -1), w_up, w_down, gain_merge.reshape(1, -1), w_merge,
         ),
-        (quad,) * 4,
     )
     east = _fetched(sw, 0, 1)
     south = _fetched(ne, 1, 0)
@@ -234,8 +292,8 @@
     own, to_east, to_south, to_corner = _call(
         shift_kernel,
         (
-            last, se, east, south, corner, _permutation(rolled, quads),
-            _permutation(quads, rolled), gain_shift.reshape(1, -1), w_qkv_shift, w_out_shift,
+            last, se, east, south, corner, shift_in, shift_out, gain_shift, w_qkv_shift,
+            w_out_shift,
         ),
         (quad,) * 4,
         smem=(0,),
@@ -246,8 +304,8 @@
     merged = _call(
         merge_kernel,
         (
-            nw, ne, sw, se, b_nw, b_ne, b_sw, own, _permutation(_merge_tokens(), quads),
-            gain_mlp.reshape(1, -1), w_up, w_down, gain_merge.reshape(1, -1), w_merge,
+            nw, ne, sw, se, b_nw, b_ne, b_sw, own, to_merge, gain_mlp, w_up, w_down, gain_merge,
+            w_merge,
         ),
         jax.ShapeDtypeStruct((QUAD // LEV, LEV, 2 * width), jnp.bfloat16),
     )

time: 44.8 us -> 37.9 us (0.85)
  waiting for transfers between devices: 14.5 us -> 8.22 us
  starting transfers between devices: 9.43 us -> 12.7 us
  Pallas kernels: 19 us -> 16.7 us
  local copies, waits for them, and re-layouts: 1.31 us -> 0 us
    pallas_call x3 -> x2, Pallas kernels: 19 us -> 7.06 us  [_call(): pl.pallas_call(kernel, out_shape=out_shape, in_specs=[pl.BlockSpec(memory...]
    pallas_call x0 -> x2, Pallas kernels: none -> 9.6 us  [the longest x1 5.07 us: on_device(): pl.pallas_call(window_kernel, out_shape=(quad,) * 4, in_specs=[pl.BlockSp...]
    ppermute x2, starting transfers between devices: 0.65 us -> 7.65 us  [_fetched(): lax.ppermute(value, 'lon', [((j + cols) % lons, j) for j in range(lons)])]
    ppermute x2, starting transfers between devices: 8.2 us -> 3.55 us  [_fetched(): return lax.ppermute(value, ('lat', 'lon'), pairs)]
    ppermute x2, waiting for transfers between devices: 10.1 us -> 5.54 us  [_fetched(): return lax.ppermute(value, ('lat', 'lon'), pairs)]
    ppermute x2, waiting for transfers between devices: 4.37 us -> 0.01 us  [_fetched(): lax.ppermute(value, 'lat', [((i + rows) % lats, i) for i in range(lats)])]
    ppermute x2, waiting for transfers between devices: 0.01 us -> 2.67 us  [_fetched(): lax.ppermute(value, 'lon', [((j + cols) % lons, j) for j in range(lons)])]
    unnamed x12 -> x0, local copies, waits for them, and re-layouts: 1.31 us -> none
  transfers between devices with their start and end apart: 6 -> 6, of which waited for: 3 -> 3; matrix products, arithmetic and copies ran while one was open for 0% -> 0% of each run, Pallas kernels for 0% -> 12%
where the time goes in v2:
time: 37.9 us; the launch traced here: 37.6 us
  Pallas kernels  16.7 us (44%)
  starting transfers between devices  12.7 us (34%)
  waiting for transfers between devices  8.22 us (22%)
    ppermute x2, starting transfers between devices, _fetched(): lax.ppermute(value, 'lon', [((j + cols) % lons, j) for j in range(lons)])  7.65 us
    pallas_call x2, Pallas kernels, _call(): pl.pallas_call(kernel, out_shape=out_shape, in_specs=[pl.BlockSpec(memory...  7.06 us
    ppermute x2, waiting for transfers between devices, _fetched(): return lax.ppermute(value, ('lat', 'lon'), pairs)  5.54 us
    pallas_call x1, Pallas kernels, on_device(): pl.pallas_call(window_kernel, out_shape=(quad,) * 4, in_specs=[pl.BlockSp...  5.07 us
    pallas_call x1, Pallas kernels, _prefetched(): pl.pallas_call(prefetch_kernel, out_shape=[pltpu.VMEM(array.shape, array....  4.54 us
    ppermute x2, starting transfers between devices, _fetched(): return lax.ppermute(value, ('lat', 'lon'), pairs)  3.55 us
    ppermute x2, waiting for transfers between devices, _fetched(): lax.ppermute(value, 'lon', [((j + cols) % lons, j) for j in range(lons)])  2.67 us
    ppermute x2, starting transfers between devices, _fetched(): lax.ppermute(value, 'lat', [((i + rows) % lats, i) for i in range(lats)])  1.5 us
  transfers between devices with their start and end apart: 6, of which 3 were waited for; matrix products, arithmetic and copies ran while one was open for 0% of the time, Pallas kernels for 12%

profile of v2, /device:TPU:6, one launch (start us, length us, event | category | flops | bytes accessed | tf_op | source)
XLA Modules:
  0.0 37.6 jit_solution(16928624270060941997)
XLA Ops:
  0.0 5.1 %shard_map.163 = (bf16[72,512]{1,0:T(8,128)(2,1)S(1)}, bf16[72,512]{1,0:T(8,128)(2,1)S(1)}, bf16[72,512]{1,0:T(8,128)(2,1)S(1)}, bf16[72,512]{1,0:T(8,128)(2,1)S(1)}) custom-call(bf16[72,4,512]{2,1,0:T(4,128)(2,1)} %bitcast.7, bf16[288,288]{1,0:T(8,128)(2,1)} %constant.18.clone.to_win_hbm, bf16[288,288]{1,0:T(8,128)(2,1)} %constant.19.clone.to_quad_hbm, ...), custom_call_target="tpu_custom_call" | custom-call | tf_op jit(solution)/shard_map/pallas_call | solution.py:269
  5.1 0.9 %collective-permute-start.1 = (bf16[72,512]{1,0:T(8,128)(2,1)S(1)}, bf16[72,512]{1,0:T(8,128)(2,1)S(1)}, u32[]{:S(2)}, u32[]{:S(2)}) collective-permute-start(bf16[72,512]{1,0:T(8,128)(2,1)S(1)} %get-tuple-element.25.a1), channel_id=1, source_target_pairs={{32,0},{64,32},{96,64},{128,96},{160,128},{192,160},{224,192},{0,2... | collective-permute-start | bytes 221192 | tf_op jit(solution)/shard_map/ppermute | solution.py:245
  6.0 7.6 %collective-permute-start = (bf16[72,512]{1,0:T(8,128)(2,1)S(1)}, bf16[72,512]{1,0:T(8,128)(2,1)S(1)}, u32[]{:S(2)}, u32[]{:S(2)}) collective-permute-start(bf16[72,512]{1,0:T(8,128)(2,1)S(1)} %get-tuple-element.26.a2), channel_id=1, source_target_pairs={{1,0},{2,1},{3,2},{4,3},{5,4},{6,5},{7,6},{8,7},{9,8},{10,9},{11,1... | collective-permute-start | bytes 221192 | tf_op jit(solution)/shard_map/ppermute | solution.py:243
  13.6 0.9 %collective-permute-start.2 = (bf16[72,512]{1,0:T(8,128)(2,1)S(1)}, bf16[72,512]{1,0:T(8,128)(2,1)S(1)}, u32[]{:S(2)}, u32[]{:S(2)}) collective-permute-start(bf16[72,512]{1,0:T(8,128)(2,1)S(1)} %get-tuple-element.24.refs_0_.a0), channel_id=1, source_target_pairs={{33,0},{34,1},{35,2},{36,3},{37,4},{38,5},{39,6},{40,7},{41,8},{42... | collective-permute-start | bytes 221192 | tf_op jit(solution)/shard_map/ppermute | solution.py:251
  14.6 4.5 %shard_map.164 = (bf16[288,288]{1,0:T(8,128)(2,1)S(1)}, bf16[288,288]{1,0:T(8,128)(2,1)S(1)}, bf16[288,288]{1,0:T(8,128)(2,1)S(1)}, f32[1,512]{1,0:T(1,128)S(1)}...) custom-call(bf16[72,512]{1,0:T(8,128)(2,1)S(1)} %get-tuple-element.2, ...), custom_call_target="tpu_custom_call" | custom-call | bytes 25165824 | tf_op jit(solution)/shard_map/pallas_call | solution.py:216
  19.1 0.0 collective-permute-done.1.c_ref
  19.1 0.0 collective-permute-done.b_ref
  19.1 0.4 %collective-permute-done.2.d_ref = bf16[72,512]{1,0:T(8,128)(2,1)S(1)} collective-permute-done((bf16[72,512]{1,0:T(8,128)(2,1)S(1)}, bf16[72,512]{1,0:T(8,128)(2,1)S(1)}, u32[]{:S(2)}, u32[]{:S(2)}) %collective-permute-start.2) | collective-permute-done | bytes 73760 | tf_op jit(solution)/shard_map/ppermute | solution.py:251
  19.5 3.3 %shard_map.165 = (bf16[72,512]{1,0:T(8,128)(2,1)S(1)}, bf16[72,512]{1,0:T(8,128)(2,1)S(1)}, bf16[72,512]{1,0:T(8,128)(2,1)S(1)}, bf16[72,512]{1,0:T(8,128)(2,1)S(1)}) custom-call(s32[1,1]{1,0:T(1,128)} %bitcast.2.last_ref, bf16[72,512]{1,0:T(8,128)(2,1)S(1)} %get-tuple-element.27.a_ref.a3, bf16[72,512]{1,0:T(8,128)(2,1)S(1)} %collective-permute-done.b_ref, ...), custom_call_target="tpu_custom_call" | custom-call | tf_op jit(solution)/shard_map/pallas_call | solution.py:228
  22.8 2.6 %collective-permute-start.3 = (bf16[72,512]{1,0:T(8,128)(2,1)S(1)}, bf16[72,512]{1,0:T(8,128)(2,1)S(1)}, u32[]{:S(2)}, u32[]{:S(2)}) collective-permute-start(bf16[72,512]{1,0:T(8,128)(2,1)S(1)} %get-tuple-element.33), channel_id=1, source_target_pairs={{255,0},{224,1},{225,2},{226,3},{227,4},{228,5},{229,6},{230,7},{2... | collective-permute-start | bytes 221192 | tf_op jit(solution)/shard_map/ppermute | solution.py:251
  25.5 0.6 %collective-permute-start.4 = (bf16[72,512]{1,0:T(8,128)(2,1)S(1)}, bf16[72,512]{1,0:T(8,128)(2,1)S(1)}, u32[]{:S(2)}, u32[]{:S(2)}) collective-permute-start(bf16[72,512]{1,0:T(8,128)(2,1)S(1)} %get-tuple-element.34), channel_id=1, source_target_pairs={{224,0},{0,32},{32,64},{64,96},{96,128},{128,160},{160,192},{192,2... | collective-permute-start | bytes 221192 | tf_op jit(solution)/shard_map/ppermute | solution.py:245
  26.1 0.0 collective-permute-start.5
  26.1 5.1 %collective-permute-done.3.b0 = bf16[72,512]{1,0:T(8,128)(2,1)S(1)} collective-permute-done((bf16[72,512]{1,0:T(8,128)(2,1)S(1)}, bf16[72,512]{1,0:T(8,128)(2,1)S(1)}, u32[]{:S(2)}, u32[]{:S(2)}) %collective-permute-start.3) | collective-permute-done | bytes 73760 | tf_op jit(solution)/shard_map/ppermute | solution.py:251
  31.2 0.0 collective-permute-done.4.b1
  31.2 2.7 %collective-permute-done.5.b2 = bf16[72,512]{1,0:T(8,128)(2,1)S(1)} collective-permute-done((bf16[72,512]{1,0:T(8,128)(2,1)S(1)}, bf16[72,512]{1,0:T(8,128)(2,1)S(1)}, u32[]{:S(2)}, u32[]{:S(2)}) %collective-permute-start.5) | collective-permute-done | bytes 73760 | tf_op jit(solution)/shard_map/ppermute | solution.py:243
  33.9 3.8 %shard_map.166 = bf16[18,4,1024]{2,1,0:T(4,128)(2,1)} custom-call(bf16[72,512]{1,0:T(8,128)(2,1)S(1)} %get-tuple-element.24.refs_0_.a0, bf16[72,512]{1,0:T(8,128)(2,1)S(1)} %get-tuple-element.25.a1, bf16[72,512]{1,0:T(8,128)(2,1)S(1)} %get-tuple-element.26.a2, bf16[72,512]{1,0:T(8,128)(2,1)S(1)} %get-tuple-element.27.a_ref.a3, ...), custom_call_target="tpu_custom_call" | custom-call | tf_op jit(solution)/shard_map/pallas_call | solution.py:228
Async XLA Ops:
  5.1 14.0 %collective-permute-start.1 = (bf16[72,512]{1,0:T(8,128)(2,1)S(1)}, bf16[72,512]{1,0:T(8,128)(2,1)S(1)}, u32[]{:S(2)}, u32[]{:S(2)}) collective-permute-start(bf16[72,512]{1,0:T(8,128)(2,1)S(1)} %get-tuple-element.25.a1), channel_id=1, source_target_pairs={{32,0},{64,32},{96,64},{128,96},{160,128},{192,160},{224,192},{0,2... | collective-permute-start | bytes 221192 | tf_op jit(solution)/shard_map/ppermute | solution.py:245
  6.0 13.1 %collective-permute-start = (bf16[72,512]{1,0:T(8,128)(2,1)S(1)}, bf16[72,512]{1,0:T(8,128)(2,1)S(1)}, u32[]{:S(2)}, u32[]{:S(2)}) collective-permute-start(bf16[72,512]{1,0:T(8,128)(2,1)S(1)} %get-tuple-element.26.a2), channel_id=1, source_target_pairs={{1,0},{2,1},{3,2},{4,3},{5,4},{6,5},{7,6},{8,7},{9,8},{10,9},{11,1... | collective-permute-start | bytes 221192 | tf_op jit(solution)/shard_map/ppermute | solution.py:243
  13.6 5.9 %collective-permute-start.2 = (bf16[72,512]{1,0:T(8,128)(2,1)S(1)}, bf16[72,512]{1,0:T(8,128)(2,1)S(1)}, u32[]{:S(2)}, u32[]{:S(2)}) collective-permute-start(bf16[72,512]{1,0:T(8,128)(2,1)S(1)} %get-tuple-element.24.refs_0_.a0), channel_id=1, source_target_pairs={{33,0},{34,1},{35,2},{36,3},{37,4},{38,5},{39,6},{40,7},{41,8},{42... | collective-permute-start | bytes 221192 | tf_op jit(solution)/shard_map/ppermute | solution.py:251
  22.8 8.4 %collective-permute-start.3 = (bf16[72,512]{1,0:T(8,128)(2,1)S(1)}, bf16[72,512]{1,0:T(8,128)(2,1)S(1)}, u32[]{:S(2)}, u32[]{:S(2)}) collective-permute-start(bf16[72,512]{1,0:T(8,128)(2,1)S(1)} %get-tuple-element.33), channel_id=1, source_target_pairs={{255,0},{224,1},{225,2},{226,3},{227,4},{228,5},{229,6},{230,7},{2... | collective-permute-start | bytes 221192 | tf_op jit(solution)/shard_map/ppermute | solution.py:251
  25.5 5.7 %collective-permute-start.4 = (bf16[72,512]{1,0:T(8,128)(2,1)S(1)}, bf16[72,512]{1,0:T(8,128)(2,1)S(1)}, u32[]{:S(2)}, u32[]{:S(2)}) collective-permute-start(bf16[72,512]{1,0:T(8,128)(2,1)S(1)} %get-tuple-element.34), channel_id=1, source_target_pairs={{224,0},{0,32},{32,64},{64,96},{96,128},{128,160},{160,192},{192,2... | collective-permute-start | bytes 221192 | tf_op jit(solution)/shard_map/ppermute | solution.py:245
  26.1 7.8 %collective-permute-start.5 = (bf16[72,512]{1,0:T(8,128)(2,1)S(1)}, bf16[72,512]{1,0:T(8,128)(2,1)S(1)}, u32[]{:S(2)}, u32[]{:S(2)}) collective-permute-start(bf16[72,512]{1,0:T(8,128)(2,1)S(1)} %get-tuple-element.35), channel_id=1, source_target_pairs={{31,0},{0,1},{1,2},{2,3},{3,4},{4,5},{5,6},{6,7},{7,8},{8,9},{9,10... | collective-permute-start | bytes 221192 | tf_op jit(solution)/shard_map/ppermute | solution.py:243

commit v3 on v1

v3 whole, which is shorter than its diff:
```python
import math

import jax
import jax.numpy as jnp
import numpy as np
from jax import lax
from jax.experimental import pallas as pl
from jax.experimental.pallas import tpu as pltpu
from jax.sharding import PartitionSpec as P

HEADS = 16
HEAD = 32
WLAT = 6
WLON = 12
WLEV = 2
LEV = 4
HALF_LAT = WLAT // 2
HALF_LON = WLON // 2
WIN = WLAT * WLON * WLEV
TOKENS = WLAT * WLON * LEV
QUAD = TOKENS // 4
GROUP = 8
LANES = GROUP * HEAD
PIECE = QUAD // 2
PAD = 40
PQUAD = 2 * PAD
PTOKENS = 4 * PQUAD
KEYS = 4 * PAD
VMEM_BYTES = 28 * 1024 * 1024
MASKED = -1e30

epsilon = 1e-05


def _natural_tokens():
    return [(r, c, l) for r in range(WLAT) for c in range(WLON) for l in range(LEV)]


def _window_tokens():
    return [(r, c, l) for l in range(LEV) for r in range(WLAT) for c in range(WLON)]


def _quadrant_tokens(odd):
    sides = (0, 1) if odd else (1, 0)
    tokens = []
    for side in sides:
        for half in range(2):
            for pair in ((1, 2), (3, 0)):
                tokens += [
                    (half * HALF_LAT + r, side * HALF_LON + c, l)
                    for l in pair
                    for r in range(HALF_LAT)
                    for c in range(HALF_LON)
                ]
                tokens += [None] * (PAD - PIECE)
    return tokens


def _merge_tokens():
    return [
        (2 * i + piece % 2, 2 * j + piece // 2, l)
        for piece in range(4)
        for i in range(WLAT // 2)
        for j in range(WLON // 2)
        for l in range(LEV)
    ]


def _permutation(target, source):
    place = {token: index for index, token in enumerate(source)}
    matrix = np.zeros((len(target), len(source)), np.float32)
    for index, token in enumerate(target):
        if token is not None:
            matrix[index, place[token]] = 1.0
    return matrix


def _bias():
    within = np.arange(KEYS) % PAD
    query = np.arange(GROUP * PAD) % PAD
    filled = np.where(within >= PIECE, MASKED, 0.0)[:, None] + np.zeros((1, GROUP * PAD))
    apart = (within >= PIECE // 2)[:, None] != (query >= PIECE // 2)[None, :]
    return np.stack([filled, filled + np.where(apart, MASKED, 0.0)]).astype(np.float32)


def normed(values, gain_row):
    centered = values - jnp.mean(values, axis=-1, keepdims=True)
    spread = jnp.mean(centered * centered, axis=-1, keepdims=True)
    return centered * lax.rsqrt(spread + epsilon) * gain_row


def dot(left, right):
    return jnp.dot(left, right, preferred_element_type=jnp.float32)


def attend(windows):
    count = windows[0][0].shape[0]
    lane = lax.broadcasted_iota(jnp.int32, (count, LANES), 1)
    heads = [
        ((lane >= h * HEAD) & (lane < (h + 1) * HEAD)).astype(jnp.float32) for h in range(GROUP)
    ]
    heads = [head.astype(windows[0][0].dtype) for head in heads]
    scale = math.log2(math.e) / math.sqrt(HEAD)
    scores = []
    for query, key, _, bias in windows:
        stacked = jnp.concatenate([query * head for head in heads], axis=0).astype(jnp.bfloat16)
        score = lax.dot_general(
            key, stacked, (((1,), (1,)), ((), ())), preferred_element_type=jnp.float32
        )
        scores.append(score if bias is None else score + bias)
    probs = []
    for score in scores:
        weights = jnp.exp2((score - jnp.max(score, axis=0, keepdims=True)) * scale)
        total = jnp.sum(weights, axis=0, keepdims=True)
        probs.append((weights * (1.0 / total)).astype(jnp.bfloat16))
    mixed = [
        lax.dot_general(
            prob, window[2], (((0,), (0,)), ((), ())), preferred_element_type=jnp.float32
        )
        for prob, window in zip(probs, windows)
    ]
    contexts = []
    for mix in mixed:
        context = mix[:count]
        for h in range(1, GROUP):
            context = jnp.where(lane >= h * HEAD, mix[h * count : (h + 1) * count], context)
        contexts.append(context)
    return contexts


def by_rows(contexts):
    per = HEADS // GROUP
    return jnp.concatenate(
        [
            jnp.concatenate(contexts[start : start + per], axis=1)
            for start in range(0, len(contexts), per)
        ],
        axis=0,
    ).astype(jnp.bfloat16)


def _fetch(pairs, sems):
    copies = [
        pltpu.make_async_copy(source, target, sems.at[index])
        for index, (source, target) in enumerate(pairs)
    ]
    for copy in copies:
        copy.start()
    return copies


def window_kernel(
    x_hbm, to_win_hbm, gain_hbm, w_qkv_hbm, w_out_hbm, to_quad_hbm, gain_shift_hbm,
    w_next_hbm, kept_ref, north_ref, south_ref, w_next_ref,
    x_ref, to_win_ref, gain_ref, w_qkv_ref, w_out_ref, to_quad_ref, gain_shift_ref, sems,
):
    odd = lax.rem(lax.axis_index("lon"), 2)
    copies = _fetch(
        (
            (x_hbm, x_ref), (to_win_hbm, to_win_ref), (gain_hbm, gain_ref),
            (w_qkv_hbm, w_qkv_ref), (w_out_hbm, w_out_ref),
            (to_quad_hbm.at[odd], to_quad_ref), (gain_shift_hbm, gain_shift_ref),
            (w_next_hbm, w_next_ref),
        ),
        sems,
    )
    for copy in copies[:3]:
        copy.wait()
    width = x_ref.shape[-1]
    x = x_ref[...].astype(jnp.float32).reshape(TOKENS, width).astype(jnp.bfloat16)
    x = dot(to_win_ref[...], x)
    tokens = normed(x, gain_ref[...]).astype(jnp.bfloat16)
    copies[3].wait()
    query, key, value = (
        dot(tokens, w_qkv_ref[:, part * width : (part + 1) * width]).astype(jnp.bfloat16)
        for part in range(3)
    )
    windows = []
    for w in range(TOKENS // WIN):
        rows = slice(w * WIN, (w + 1) * WIN)
        for g in range(HEADS // GROUP):
            cols = slice(g * LANES, (g + 1) * LANES)
            windows.append((query[rows, cols], key[rows, cols], value[rows, cols], None))
    context = by_rows(attend(windows))
    for copy in copies[4:7]:
        copy.wait()
    after = (x + dot(context, w_out_ref[...])).astype(jnp.bfloat16)
    after = dot(to_quad_ref[...], after)
    kept_ref[...] = after.astype(jnp.bfloat16)
    quads = normed(after, gain_shift_ref[...]).astype(jnp.bfloat16)
    for half, ref in enumerate((north_ref, south_ref)):
        ref[:PQUAD] = quads[half * PQUAD : (half + 1) * PQUAD]
        ref[PQUAD:] = quads[(2 + half) * PQUAD : (3 + half) * PQUAD]
    copies[7].wait()


def own_kernel(
    north_ref, south_ref, w_qkv_ref, bias_hbm,
    query_ref, kv_ref, side_a_ref, side_b_ref, bias_ref, sems,
):
    copies = _fetch(((bias_hbm, bias_ref),), sems)
    side_a = jnp.concatenate([north_ref[:PQUAD], south_ref[:PQUAD]], axis=0)
    side_b = jnp.concatenate([north_ref[PQUAD:], south_ref[PQUAD:]], axis=0)
    side_a_ref[...] = side_a
    side_b_ref[...] = side_b
    tokens = jnp.concatenate([side_a, side_b], axis=0)
    width = tokens.shape[-1]
    query_ref[...] = dot(tokens, w_qkv_ref[:, :width])
    kv_ref[...] = dot(tokens, w_qkv_ref[:, width:])
    copies[0].wait()


def side_context(side, query_ref, kv_ref, kv_near_ref, kv_corner_ref, bias_ref):
    width = query_ref.shape[-1]
    band = lax.axis_index("lat")
    place = lax.broadcasted_iota(jnp.int32, (KEYS, GROUP * PAD), 0)
    across = ((place >= PAD) & (place < 2 * PAD)) | (place >= 3 * PAD)
    windows = []
    for half in range(2):
        edge = band == (0 if half == 0 else lax.axis_size("lat") - 1)
        seam = jnp.where(across & edge, jnp.float32(MASKED), jnp.float32(0.0))
        own = (side * 2 + half) * PQUAD
        for pair in range(2):
            bias = bias_ref[pair] + seam
            at = pair * PAD
            kv = jnp.concatenate(
                [
                    ref[start + at : start + at + PAD]
                    for ref, start in (
                        (kv_ref, own), (kv_near_ref, half * PQUAD),
                        (kv_near_ref, (2 + half) * PQUAD), (kv_corner_ref, half * PQUAD),
                    )
                ],
                axis=0,
            ).astype(jnp.bfloat16)
            query = query_ref[own + at : own + at + PAD]
            for g in range(HEADS // GROUP):
                cols = slice(g * LANES, (g + 1) * LANES)
                values = slice(width + g * LANES, width + (g + 1) * LANES)
                windows.append((query[:, cols], kv[:, cols], kv[:, values], bias))
    return by_rows(attend(windows))


def near_kernel(
    north_ref, south_ref, side_a_ref, side_b_ref, corner_ref, query_ref, kv_ref, w_qkv_ref,
    bias_ref, context_ref, kv_b_ref, kv_a_ref, kv_corner_ref,
):
    width = query_ref.shape[-1]
    w_kv = w_qkv_ref[:, width:]
    kv_a_ref[...] = dot(
        jnp.concatenate([north_ref[:PQUAD], south_ref[:PQUAD], side_a_ref[...]], axis=0), w_kv
    )
    kv_corner_ref[...] = dot(corner_ref[...], w_kv)
    kv_b_ref[...] = dot(
        jnp.concatenate([north_ref[PQUAD:], south_ref[PQUAD:], side_b_ref[...]], axis=0), w_kv
    )
    context_ref[...] = side_context(0, query_ref, kv_ref, kv_a_ref, kv_corner_ref, bias_ref)


def last_kernel(
    corner_ref, kept_ref, context_ref, query_ref, kv_ref, kv_b_ref, w_qkv_ref, bias_ref,
    w_out_hbm, gain_mlp_hbm, w_up_hbm, w_down_hbm, to_merge_hbm, gain_merge_hbm, w_merge_hbm,
    out_ref, kv_corner_ref,
    w_out_ref, gain_mlp_ref, w_up_ref, w_down_ref, to_merge_ref, gain_merge_ref, w_merge_ref, sems,
):
    odd = lax.rem(lax.axis_index("lon"), 2)
    copies = _fetch(
        (
            (w_out_hbm, w_out_ref), (gain_mlp_hbm, gain_mlp_ref), (w_up_hbm, w_up_ref),
            (w_down_hbm, w_down_ref), (to_merge_hbm.at[odd], to_merge_ref),
            (gain_merge_hbm, gain_merge_ref), (w_merge_hbm, w_merge_ref),
        ),
        sems,
    )
    width = kept_ref.shape[-1]
    kv_corner_ref[...] = dot(corner_ref[...], w_qkv_ref[:, width:])
    context = side_context(1, query_ref, kv_ref, kv_b_ref, kv_corner_ref, bias_ref)
    context = jnp.concatenate([context_ref[...], context], axis=0)
    copies[0].wait()
    branch = dot(context, w_out_ref[...]).astype(jnp.bfloat16).astype(jnp.float32)
    copies[1].wait()
    shift = (kept_ref[...].astype(jnp.float32) + branch).astype(jnp.bfloat16).astype(jnp.float32)
    tokens = normed(shift, gain_mlp_ref[...]).astype(jnp.bfloat16)
    copies[2].wait()
    hidden = jax.nn.gelu(dot(tokens, w_up_ref[...]), approximate=True).astype(jnp.bfloat16)
    copies[3].wait()
    after = (shift + dot(hidden, w_down_ref[...])).astype(jnp.bfloat16)
    copies[4].wait()
    merge = dot(to_merge_ref[...], after)
    stacked = jnp.concatenate([merge[i * QUAD : (i + 1) * QUAD] for i in range(4)], axis=1)
    copies[5].wait()
    tokens = normed(stacked, gain_merge_ref[...]).astype(jnp.bfloat16)
    copies[6].wait()
    merged = dot(tokens, w_merge_ref[...])
    out_ref[...] = merged.reshape(out_ref.shape).astype(jnp.bfloat16)


def _in_hbm(array):
    return pltpu.with_memory_space_constraint(array, pltpu.HBM)


def _call(kernel, near, far, outs, scratch=(), copies=0, flops=0):
    near_spec, far_spec = pl.BlockSpec(memory_space=pltpu.VMEM), pl.BlockSpec(memory_space=pltpu.HBM)
    return pl.pallas_call(
        kernel,
        out_shape=outs,
        in_specs=[near_spec] * len(near) + [far_spec] * len(far),
        out_specs=jax.tree.map(lambda _: near_spec, outs),
        scratch_shapes=list(scratch) + ([pltpu.SemaphoreType.DMA((copies,))] if copies else []),
        compiler_params=pltpu.CompilerParams(vmem_limit_bytes=VMEM_BYTES),
        cost_estimate=pl.CostEstimate(flops=flops, bytes_accessed=0, transcendentals=0),
    )(*near, *map(_in_hbm, far))


def _vmem(array):
    return pltpu.VMEM(array.shape, array.dtype)


def _rows(value, step):
    count = lax.axis_size("lat")
    return lax.ppermute(value, "lat", [((i + step) % count, i) for i in range(count)])


def _swap(value, first):
    count = lax.axis_size("lon")
    pairs = [(j % count, (j + 1) % count) for j in range(first, count + first, 2)]
    return lax.ppermute(value, "lon", pairs + [(b, a) for a, b in pairs])


def on_device(
    latent_field, gain_win, w_qkv_win, w_out_win, gain_shift, w_qkv_shift, w_out_shift,
    gain_mlp, w_up, w_down, gain_merge, w_merge,
):
    width = latent_field.shape[-1]
    natural, windows, merges = _natural_tokens(), _window_tokens(), _merge_tokens()
    quads = [_quadrant_tokens(odd) for odd in (False, True)]
    to_win = jnp.asarray(_permutation(windows, natural), jnp.bfloat16)
    to_quad = jnp.asarray(np.stack([_permutation(q, windows) for q in quads]), jnp.bfloat16)
    to_merge = jnp.asarray(np.stack([_permutation(merges, q) for q in quads]), jnp.bfloat16)
    bias = jnp.asarray(_bias())
    gain_win, gain_shift, gain_mlp, gain_merge = (
        gain.reshape(1, -1) for gain in (gain_win, gain_shift, gain_mlp, gain_merge)
    )

    def bf16(rows, cols=width):
        return pltpu.VMEM((rows, cols), jnp.bfloat16)

    def f32(rows, cols):
        return pltpu.VMEM((rows, cols), jnp.float32)

    x = latent_field.reshape(WLAT * WLON, LEV, width)
    first = (x, to_win, gain_win, w_qkv_win, w_out_win, to_quad, gain_shift, w_qkv_shift)
    held = [_vmem(array) for array in first[:-1]]
    held[5] = bf16(PTOKENS, TOKENS)
    kept, north, south, w_qkv = _call(
        window_kernel, (), first,
        (bf16(PTOKENS), bf16(2 * PQUAD), bf16(2 * PQUAD), _vmem(w_qkv_shift)), held, len(first),
    )
    from_north = _rows(south, -1)
    from_south = _rows(north, 1)
    query, kv, side_a, side_b, bias = _call(
        own_kernel, (north, south, w_qkv), (bias,),
        (
            f32(PTOKENS, width), f32(PTOKENS, 2 * width), bf16(2 * PQUAD), bf16(2 * PQUAD),
            _vmem(bias),
        ),
        copies=1,
    )
    from_a = _swap(side_a, 0)
    from_b = _swap(side_b, 1)
    corner_a = _swap(jnp.concatenate([from_north[:PQUAD], from_south[:PQUAD]], axis=0), 0)
    corner_b = _swap(jnp.concatenate([from_north[PQUAD:], from_south[PQUAD:]], axis=0), 1)
    context, kv_b = _call(
        near_kernel,
        (from_north, from_south, from_a, from_b, corner_a, query, kv, w_qkv, bias), (),
        (bf16(2 * PQUAD), f32(4 * PQUAD, 2 * width)),
        (f32(4 * PQUAD, 2 * width), f32(2 * PQUAD, 2 * width)), flops=10**11,
    )
    far = (w_out_shift, gain_mlp, w_up, w_down, to_merge, gain_merge, w_merge)
    held = [_vmem(array) for array in far]
    held[4] = bf16(TOKENS, PTOKENS)
    merged = _call(
        last_kernel, (corner_b, kept, context, query, kv, kv_b, w_qkv, bias), far,
        jax.ShapeDtypeStruct((QUAD // LEV, LEV, 2 * width), jnp.bfloat16),
        [f32(2 * PQUAD, 2 * width)] + held, len(far),
    )
    return merged.reshape(WLAT // 2, WLON // 2, LEV, 2 * width)


def solution(mesh):
    in_specs = (P("lat", "lon", None, None),) + (P(),) * 11
    return jax.shard_map(
        on_device,
        mesh=mesh,
        in_specs=in_specs,
        out_specs=P("lat", "lon", None, None),
        check_vma=False,
    )
```

time: 44.8 us -> 33.9 us (0.76)
  the two profiles are of different devices: /device:TPU:6 before, /device:TPU:8 now
where the time goes in v3:
time: 33.9 us; the launch traced here: 33.8 us
  starting transfers between devices  15.1 us (45%)
  Pallas kernels  14.9 us (44%)
  waiting for transfers between devices  3.53 us (10%)
    pallas_call x4, Pallas kernels, _call(): pl.pallas_call(kernel, out_shape=outs, in_specs=[near_spec] * len(near) +...  14.9 us
    ppermute x4, starting transfers between devices, _swap(): return lax.ppermute(value, 'lon', pairs + [(b, a) for a, b in pairs])  10.9 us
    ppermute x2, starting transfers between devices, _rows(): lax.ppermute(value, 'lat', [((i + step) % count, i) for i in range(count)])  4.21 us
    ppermute x4, waiting for transfers between devices, _swap(): return lax.ppermute(value, 'lon', pairs + [(b, a) for a, b in pairs])  3.52 us
  transfers between devices with their start and end apart: 6, of which 1 were waited for; matrix products, arithmetic and copies ran while one was open for 0% of the time, Pallas kernels for 9%

profile of v3, /device:TPU:8, one launch (start us, length us, event | category | flops | bytes accessed | tf_op | source)
XLA Modules:
  0.0 33.8 jit_solution(16179965657234907315)
XLA Ops:
  0.0 4.5 %shard_map.154 = (bf16[320,512]{1,0:T(8,128)(2,1)S(1)}, bf16[160,512]{1,0:T(8,128)(2,1)S(1)}, bf16[160,512]{1,0:T(8,128)(2,1)S(1)}, bf16[512,1536]{1,0:T(8,128)(2,1)S(1)}) custom-call(bf16[72,4,512]{2,1,0:T(4,128)(2,1)} %bitcast.6, bf16[288,288]{1,0:T(8,128)(2,1)} %constant.8.clone.to_win_hbm, f32[1,512]{1,0:T(1,128)} %bitcast.8, ...), custom_call_target="tpu_custom_call" | custom-call | tf_op jit(solution)/shard_map/pallas_call | solution.py:304
  4.5 1.6 %collective-permute-start = (bf16[160,512]{1,0:T(8,128)(2,1)S(1)}, bf16[160,512]{1,0:T(8,128)(2,1)S(1)}, u32[]{:S(2)}, u32[]{:S(2)}) collective-permute-start(bf16[160,512]{1,0:T(8,128)(2,1)S(1)} %get-tuple-element.16.south_ref), channel_id=1, source_target_pairs={{224,0},{0,32},{32,64},{64,96},{96,128},{128,160},{160,192},{192,2... | collective-permute-start | bytes 491528 | tf_op jit(solution)/shard_map/ppermute | solution.py:321
  6.1 2.6 %collective-permute-start.1 = (bf16[160,512]{1,0:T(8,128)(2,1)S(1)}, bf16[160,512]{1,0:T(8,128)(2,1)S(1)}, u32[]{:S(2)}, u32[]{:S(2)}) collective-permute-start(bf16[160,512]{1,0:T(8,128)(2,1)S(1)} %get-tuple-element.17.north_ref), channel_id=1, source_target_pairs={{32,0},{64,32},{96,64},{128,96},{160,128},{192,160},{224,192},{0,2... | collective-permute-start | bytes 491528 | tf_op jit(solution)/shard_map/ppermute | solution.py:321
  8.7 1.0 %shard_map.155 = (f32[320,512]{1,0:T(8,128)S(1)}, f32[320,1024]{1,0:T(8,128)S(1)}, bf16[160,512]{1,0:T(8,128)(2,1)S(1)}, bf16[160,512]{1,0:T(8,128)(2,1)S(1)}, f32[2,160,320]{2,1,0:T(8,128)S(1)}) custom-call(bf16[160,512]{1,0:T(8,128)(2,1)S(1)} %get-tuple-element.17.north_ref, bf16[160,512]{1,0:T(8,128)(2,1)S(1)} %get-tuple-element.16.south_ref, ...), custom_call_target="tpu_custom_call" | custom-call | tf_op jit(solution)/shard_map/pallas_call | solution.py:304
  9.8 0.1 collective-permute-start.3
  9.9 7.7 %collective-permute-start.4 = (bf16[160,512]{1,0:T(8,128)(2,1)S(1)}, bf16[160,512]{1,0:T(8,128)(2,1)S(1)}, u32[]{:S(2)}, u32[]{:S(2)}) collective-permute-start(bf16[160,512]{1,0:T(8,128)(2,1)S(1)} %get-tuple-element.21), channel_id=1, source_target_pairs={{1,2},{3,4},{5,6},{7,8},{9,10},{11,12},{13,14},{15,16},{17,18},{19... | collective-permute-start | bytes 491528 | tf_op jit(solution)/shard_map/ppermute | solution.py:327
  17.6 0.0 collective-permute-done.north_ref
  17.6 0.0 collective-permute-done.1.south_ref
  17.6 0.1 collective-permute-start.5
  17.8 3.0 %collective-permute-start.2 = (bf16[160,512]{1,0:T(8,128)(2,1)S(1)}, bf16[160,512]{1,0:T(8,128)(2,1)S(1)}, u32[]{:S(2)}, u32[]{:S(2)}) collective-permute-start(bf16[160,512]{1,0:T(8,128)(2,1)S(1)} %pad_maximum_fusion), channel_id=1, source_target_pairs={{1,2},{3,4},{5,6},{7,8},{9,10},{11,12},{13,14},{15,16},{17,18},{19... | collective-permute-start | bytes 491528 | tf_op jit(solution)/shard_map/ppermute | solution.py:327
  20.8 0.0 collective-permute-done.3.side_a_ref
  20.8 0.0 collective-permute-done.4.side_b_ref
  20.8 0.0 collective-permute-done.5.corner_ref
  20.8 2.1 %shard_map.156 = (bf16[160,512]{1,0:T(8,128)(2,1)S(1)}, f32[320,1024]{1,0:T(8,128)S(1)}) custom-call(bf16[160,512]{1,0:T(8,128)(2,1)S(1)} %collective-permute-done.north_ref, bf16[160,512]{1,0:T(8,128)(2,1)S(1)} %collective-permute-done.1.south_ref, bf16[160,512]{1,0:T(8,128)(2,1)S(1)} %collective-permute-done.3.side_a_ref, ...), custom_call_target="tpu_custom_call" | custom-call | flops 99999997952 | tf_op jit(solution)/shard_map/pallas_call | solution.py:304
  22.9 3.5 %collective-permute-done.2.corner_ref = bf16[160,512]{1,0:T(8,128)(2,1)S(1)} collective-permute-done((bf16[160,512]{1,0:T(8,128)(2,1)S(1)}, bf16[160,512]{1,0:T(8,128)(2,1)S(1)}, u32[]{:S(2)}, u32[]{:S(2)}) %collective-permute-start.2) | collective-permute-done | bytes 163872 | tf_op jit(solution)/shard_map/ppermute | solution.py:327
  26.4 7.2 %shard_map.157 = bf16[18,4,1024]{2,1,0:T(4,128)(2,1)} custom-call(bf16[160,512]{1,0:T(8,128)(2,1)S(1)} %collective-permute-done.2.corner_ref, bf16[320,512]{1,0:T(8,128)(2,1)S(1)} %get-tuple-element.18.kept_ref, bf16[160,512]{1,0:T(8,128)(2,1)S(1)} %get-tuple-element.25.context_ref, f32[320,512]{1,0:T(8,128)S(1)} %get-tuple-element.22.query_ref, ...), custom_call_target="tpu_custom_call" | custom-call | tf_op jit(solution)/shard_map/pallas_call | solution.py:304
  (4 shorter events, 0.1 us)
Async XLA Ops:
  4.5 13.1 %collective-permute-start = (bf16[160,512]{1,0:T(8,128)(2,1)S(1)}, bf16[160,512]{1,0:T(8,128)(2,1)S(1)}, u32[]{:S(2)}, u32[]{:S(2)}) collective-permute-start(bf16[160,512]{1,0:T(8,128)(2,1)S(1)} %get-tuple-element.16.south_ref), channel_id=1, source_target_pairs={{224,0},{0,32},{32,64},{64,96},{96,128},{128,160},{160,192},{192,2... | collective-permute-start | bytes 491528 | tf_op jit(solution)/shard_map/ppermute | solution.py:321
  6.1 11.5 %collective-permute-start.1 = (bf16[160,512]{1,0:T(8,128)(2,1)S(1)}, bf16[160,512]{1,0:T(8,128)(2,1)S(1)}, u32[]{:S(2)}, u32[]{:S(2)}) collective-permute-start(bf16[160,512]{1,0:T(8,128)(2,1)S(1)} %get-tuple-element.17.north_ref), channel_id=1, source_target_pairs={{32,0},{64,32},{96,64},{128,96},{160,128},{192,160},{224,192},{0,2... | collective-permute-start | bytes 491528 | tf_op jit(solution)/shard_map/ppermute | solution.py:321
  9.8 11.0 %collective-permute-start.3 = (bf16[160,512]{1,0:T(8,128)(2,1)S(1)}, bf16[160,512]{1,0:T(8,128)(2,1)S(1)}, u32[]{:S(2)}, u32[]{:S(2)}) collective-permute-start(bf16[160,512]{1,0:T(8,128)(2,1)S(1)} %get-tuple-element.20), channel_id=1, source_target_pairs={{0,1},{2,3},{4,5},{6,7},{8,9},{10,11},{12,13},{14,15},{16,17},{18,... | collective-permute-start | bytes 491528 | tf_op jit(solution)/shard_map/ppermute | solution.py:327
  9.9 10.9 %collective-permute-start.4 = (bf16[160,512]{1,0:T(8,128)(2,1)S(1)}, bf16[160,512]{1,0:T(8,128)(2,1)S(1)}, u32[]{:S(2)}, u32[]{:S(2)}) collective-permute-start(bf16[160,512]{1,0:T(8,128)(2,1)S(1)} %get-tuple-element.21), channel_id=1, source_target_pairs={{1,2},{3,4},{5,6},{7,8},{9,10},{11,12},{13,14},{15,16},{17,18},{19... | collective-permute-start | bytes 491528 | tf_op jit(solution)/shard_map/ppermute | solution.py:327
  17.6 3.1 %collective-permute-start.5 = (bf16[160,512]{1,0:T(8,128)(2,1)S(1)}, bf16[160,512]{1,0:T(8,128)(2,1)S(1)}, u32[]{:S(2)}, u32[]{:S(2)}) collective-permute-start(bf16[160,512]{1,0:T(8,128)(2,1)S(1)} %pad_maximum_fusion.1), channel_id=1, source_target_pairs={{0,1},{2,3},{4,5},{6,7},{8,9},{10,11},{12,13},{14,15},{16,17},{18,... | collective-permute-start | bytes 491528 | tf_op jit(solution)/shard_map/ppermute | solution.py:327
  17.8 8.6 %collective-permute-start.2 = (bf16[160,512]{1,0:T(8,128)(2,1)S(1)}, bf16[160,512]{1,0:T(8,128)(2,1)S(1)}, u32[]{:S(2)}, u32[]{:S(2)}) collective-permute-start(bf16[160,512]{1,0:T(8,128)(2,1)S(1)} %pad_maximum_fusion), channel_id=1, source_target_pairs={{1,2},{3,4},{5,6},{7,8},{9,10},{11,12},{13,14},{15,16},{17,18},{19... | collective-permute-start | bytes 491528 | tf_op jit(solution)/shard_map/ppermute | solution.py:327

commit v4 on v3

--- a/solution.py
+++ b/solution.py
@@ -22,10 +22,9 @@
 GROUP = 8
 LANES = GROUP * HEAD
 PIECE = QUAD // 2
-PAD = 40
-PQUAD = 2 * PAD
-PTOKENS = 4 * PQUAD
-KEYS = 4 * PAD
+SLOT = 40
+KEYS = 4 * PIECE
+HALF = 2 * QUAD
 VMEM_BYTES = 28 * 1024 * 1024
 MASKED = -1e30
 
@@ -52,7 +51,6 @@
                     for r in range(HALF_LAT)
                     for c in range(HALF_LON)
                 ]
-                tokens += [None] * (PAD - PIECE)
     return tokens
 
 
@@ -70,17 +68,14 @@
     place = {token: index for index, token in enumerate(source)}
     matrix = np.zeros((len(target), len(source)), np.float32)
     for index, token in enumerate(target):
-        if token is not None:
-            matrix[index, place[token]] = 1.0
+        matrix[index, place[token]] = 1.0
     return matrix
 
 
 def _bias():
-    within = np.arange(KEYS) % PAD
-    query = np.arange(GROUP * PAD) % PAD
-    filled = np.where(within >= PIECE, MASKED, 0.0)[:, None] + np.zeros((1, GROUP * PAD))
-    apart = (within >= PIECE // 2)[:, None] != (query >= PIECE // 2)[None, :]
-    return np.stack([filled, filled + np.where(apart, MASKED, 0.0)]).astype(np.float32)
+    key = np.arange(KEYS) % PIECE >= PIECE // 2
+    query = np.arange(GROUP * SLOT) % SLOT >= PIECE // 2
+    return np.where(key[:, None] != query[None, :], MASKED, 0.0).astype(np.float32)
 
 
 def normed(values, gain_row):
@@ -128,15 +123,24 @@
     return contexts
 
 
-def by_rows(contexts):
+def by_rows(contexts, count):
     per = HEADS // GROUP
     return jnp.concatenate(
         [
-            jnp.concatenate(contexts[start : start + per], axis=1)
+            jnp.concatenate(contexts[start : start + per], axis=1)[:count]
             for start in range(0, len(contexts), per)
         ],
         axis=0,
     ).astype(jnp.bfloat16)
+
+
+def halves(ref):
+    values = ref[...].astype(jnp.float32)
+    return values[:QUAD], values[QUAD:]
+
+
+def rounded(*parts):
+    return jnp.concatenate(parts, axis=0).astype(jnp.bfloat16)
 
 
 def _fetch(pairs, sems):
@@ -181,16 +185,17 @@
         for g in range(HEADS // GROUP):
             cols = slice(g * LANES, (g + 1) * LANES)
             windows.append((query[rows, cols], key[rows, cols], value[rows, cols], None))
-    context = by_rows(attend(windows))
+    context = by_rows(attend(windows), WIN)
     for copy in copies[4:7]:
         copy.wait()
     after = (x + dot(context, w_out_ref[...])).astype(jnp.bfloat16)
     after = dot(to_quad_ref[...], after)
     kept_ref[...] = after.astype(jnp.bfloat16)
-    quads = normed(after, gain_shift_ref[...]).astype(jnp.bfloat16)
+    quads = normed(after, gain_shift_ref[...])
     for half, ref in enumerate((north_ref, south_ref)):
-        ref[:PQUAD] = quads[half * PQUAD : (half + 1) * PQUAD]
-        ref[PQUAD:] = quads[(2 + half) * PQUAD : (3 + half) * PQUAD]
+        ref[...] = rounded(
+            *(quads[start : start + QUAD] for start in (half * QUAD, HALF + half * QUAD))
+        )
     copies[7].wait()
 
 
@@ -199,13 +204,14 @@
     query_ref, kv_ref, side_a_ref, side_b_ref, bias_ref, sems,
 ):
     copies = _fetch(((bias_hbm, bias_ref),), sems)
-    side_a = jnp.concatenate([north_ref[:PQUAD], south_ref[:PQUAD]], axis=0)
-    side_b = jnp.concatenate([north_ref[PQUAD:], south_ref[PQUAD:]], axis=0)
+    (na, nb), (sa, sb) = halves(north_ref), halves(south_ref)
+    side_a, side_b = rounded(na, sa), rounded(nb, sb)
     side_a_ref[...] = side_a
     side_b_ref[...] = side_b
     tokens = jnp.concatenate([side_a, side_b], axis=0)
     width = tokens.shape[-1]
-    query_ref[...] = dot(tokens, w_qkv_ref[:, :width])
+    query_ref[:TOKENS] = dot(tokens, w_qkv_ref[:, :width])
+    query_ref[TOKENS:] = jnp.zeros_like(query_ref[TOKENS:])
     kv_ref[...] = dot(tokens, w_qkv_ref[:, width:])
     copies[0].wait()
 
@@ -213,84 +219,98 @@
 def side_context(side, query_ref, kv_ref, kv_near_ref, kv_corner_ref, bias_ref):
     width = query_ref.shape[-1]
     band = lax.axis_index("lat")
-    place = lax.broadcasted_iota(jnp.int32, (KEYS, GROUP * PAD), 0)
-    across = ((place >= PAD) & (place < 2 * PAD)) | (place >= 3 * PAD)
+    place = lax.broadcasted_iota(jnp.int32, (KEYS, GROUP * SLOT), 0)
+    across = ((place >= PIECE) & (place < 2 * PIECE)) | (place >= 3 * PIECE)
     windows = []
     for half in range(2):
         edge = band == (0 if half == 0 else lax.axis_size("lat") - 1)
         seam = jnp.where(across & edge, jnp.float32(MASKED), jnp.float32(0.0))
-        own = (side * 2 + half) * PQUAD
+        own = side * HALF + half * QUAD
         for pair in range(2):
-            bias = bias_ref[pair] + seam
-            at = pair * PAD
-            kv = jnp.concatenate(
-                [
-                    ref[start + at : start + at + PAD]
+            bias = seam if pair == 0 else seam + bias_ref[...]
+            at = pair * PIECE
+            kv = rounded(
+                *(
+                    ref[start + at : start + at + PIECE]
                     for ref, start in (
-                        (kv_ref, own), (kv_near_ref, half * PQUAD),
-                        (kv_near_ref, (2 + half) * PQUAD), (kv_corner_ref, half * PQUAD),
+                        (kv_ref, own), (kv_near_ref, half * QUAD),
+                        (kv_near_ref, HALF + half * QUAD), (kv_corner_ref, half * QUAD),
                     )
-                ],
-                axis=0,
-            ).astype(jnp.bfloat16)
-            query = query_ref[own + at : own + at + PAD]
+                )
+            )
+            query = query_ref[own + at : own + at + SLOT]
             for g in range(HEADS // GROUP):
                 cols = slice(g * LANES, (g + 1) * LANES)
                 values = slice(width + g * LANES, width + (g + 1) * LANES)
                 windows.append((query[:, cols], kv[:, cols], kv[:, values], bias))
-    return by_rows(attend(windows))
+    return by_rows(attend(windows), PIECE)
+
+
+def block(context, kept, w_out, gain_mlp, w_up, w_down):
+    branch = dot(context, w_out()).astype(jnp.bfloat16).astype(jnp.float32)
+    shift = (kept.astype(jnp.float32) + branch).astype(jnp.bfloat16).astype(jnp.float32)
+    tokens = normed(shift, gain_mlp()).astype(jnp.bfloat16)
+    hidden = jax.nn.gelu(dot(tokens, w_up()), approximate=True).astype(jnp.bfloat16)
+    return (shift + dot(hidden, w_down())).astype(jnp.bfloat16)
 
 
 def near_kernel(
-    north_ref, south_ref, side_a_ref, side_b_ref, corner_ref, query_ref, kv_ref, w_qkv_ref,
-    bias_ref, context_ref, kv_b_ref, kv_a_ref, kv_corner_ref,
+    north_ref, south_ref, side_a_ref, side_b_ref, corner_ref, kept_ref, query_ref, kv_ref,
+    w_qkv_ref, bias_ref, w_out_hbm, gain_mlp_hbm, w_up_hbm, w_down_hbm,
+    after_ref, kv_b_ref, w_out_ref, gain_mlp_ref, w_up_ref, w_down_ref,
+    kv_a_ref, kv_corner_ref, sems,
 ):
+    pairs = (
+        (w_out_hbm, w_out_ref), (gain_mlp_hbm, gain_mlp_ref), (w_up_hbm, w_up_ref),
+        (w_down_hbm, w_down_ref),
+    )
+    copies = _fetch(pairs, sems)
+
+    def arrived(index):
+        def array():
+            copies[index].wait()
+            return pairs[index][1][...]
+
+        return array
+
     width = query_ref.shape[-1]
     w_kv = w_qkv_ref[:, width:]
-    kv_a_ref[...] = dot(
-        jnp.concatenate([north_ref[:PQUAD], south_ref[:PQUAD], side_a_ref[...]], axis=0), w_kv
-    )
+    (north_a, north_b), (south_a, south_b) = halves(north_ref), halves(south_ref)
+    kv_a_ref[:HALF] = dot(rounded(north_a, south_a), w_kv)
+    kv_a_ref[HALF:] = dot(side_a_ref[...], w_kv)
     kv_corner_ref[...] = dot(corner_ref[...], w_kv)
-    kv_b_ref[...] = dot(
-        jnp.concatenate([north_ref[PQUAD:], south_ref[PQUAD:], side_b_ref[...]], axis=0), w_kv
-    )
-    context_ref[...] = side_context(0, query_ref, kv_ref, kv_a_ref, kv_corner_ref, bias_ref)
+    kv_b_ref[:HALF] = dot(rounded(north_b, south_b), w_kv)
+    kv_b_ref[HALF:] = dot(side_b_ref[...], w_kv)
+    context = side_context(0, query_ref, kv_ref, kv_a_ref, kv_corner_ref, bias_ref)
+    after_ref[...] = block(context, kept_ref[:HALF], *map(arrived, range(4)))
 
 
 def last_kernel(
-    corner_ref, kept_ref, context_ref, query_ref, kv_ref, kv_b_ref, w_qkv_ref, bias_ref,
-    w_out_hbm, gain_mlp_hbm, w_up_hbm, w_down_hbm, to_merge_hbm, gain_merge_hbm, w_merge_hbm,
-    out_ref, kv_corner_ref,
-    w_out_ref, gain_mlp_ref, w_up_ref, w_down_ref, to_merge_ref, gain_merge_ref, w_merge_ref, sems,
+    corner_ref, kept_ref, after_ref, query_ref, kv_ref, kv_b_ref, w_qkv_ref, bias_ref,
+    w_out_ref, gain_mlp_ref, w_up_ref, w_down_ref, to_merge_hbm, gain_merge_hbm, w_merge_hbm,
+    out_ref, kv_corner_ref, to_merge_ref, gain_merge_ref, w_merge_ref, sems,
 ):
     odd = lax.rem(lax.axis_index("lon"), 2)
     copies = _fetch(
         (
-            (w_out_hbm, w_out_ref), (gain_mlp_hbm, gain_mlp_ref), (w_up_hbm, w_up_ref),
-            (w_down_hbm, w_down_ref), (to_merge_hbm.at[odd], to_merge_ref),
-            (gain_merge_hbm, gain_merge_ref), (w_merge_hbm, w_merge_ref),
+            (to_merge_hbm.at[odd], to_merge_ref), (gain_merge_hbm, gain_merge_ref),
+            (w_merge_hbm, w_merge_ref),
         ),
         sems,
     )
     width = kept_ref.shape[-1]
     kv_corner_ref[...] = dot(corner_ref[...], w_qkv_ref[:, width:])
     context = side_context(1, query_ref, kv_ref, kv_b_ref, kv_corner_ref, bias_ref)
-    context = jnp.concatenate([context_ref[...], context], axis=0)
+    weights = (w_out_ref, gain_mlp_ref, w_up_ref, w_down_ref)
+    after = block(
+        context, kept_ref[HALF:], *(lambda ref=ref: ref[...] for ref in weights)
+    )
     copies[0].wait()
-    branch = dot(context, w_out_ref[...]).astype(jnp.bfloat16).astype(jnp.float32)
+    merge = dot(to_merge_ref[...], jnp.concatenate([after_ref[...], after], axis=0))
+    stacked = jnp.concatenate([merge[i * QUAD : (i + 1) * QUAD] for i in range(4)], axis=1)
     copies[1].wait()
-    shift = (kept_ref[...].astype(jnp.float32) + branch).astype(jnp.bfloat16).astype(jnp.float32)
-    tokens = normed(shift, gain_mlp_ref[...]).astype(jnp.bfloat16)
+    tokens = normed(stacked, gain_merge_ref[...]).astype(jnp.bfloat16)
     copies[2].wait()
-    hidden = jax.nn.gelu(dot(tokens, w_up_ref[...]), approximate=True).astype(jnp.bfloat16)
-    copies[3].wait()
-    after = (shift + dot(hidden, w_down_ref[...])).astype(jnp.bfloat16)
-    copies[4].wait()
-    merge = dot(to_merge_ref[...], after)
-    stacked = jnp.concatenate([merge[i * QUAD : (i + 1) * QUAD] for i in range(4)], axis=1)
-    copies[5].wait()
-    tokens = normed(stacked, gain_merge_ref[...]).astype(jnp.bfloat16)
-    copies[6].wait()
     merged = dot(tokens, w_merge_ref[...])
     out_ref[...] = merged.reshape(out_ref.shape).astype(jnp.bfloat16)
 
@@ -351,38 +371,40 @@
     x = latent_field.reshape(WLAT * WLON, LEV, width)
     first = (x, to_win, gain_win, w_qkv_win, w_out_win, to_quad, gain_shift, w_qkv_shift)
     held = [_vmem(array) for array in first[:-1]]
-    held[5] = bf16(PTOKENS, TOKENS)
+    held[5] = bf16(TOKENS, TOKENS)
     kept, north, south, w_qkv = _call(
         window_kernel, (), first,
-        (bf16(PTOKENS), bf16(2 * PQUAD), bf16(2 * PQUAD), _vmem(w_qkv_shift)), held, len(first),
+        (bf16(TOKENS), bf16(HALF), bf16(HALF), _vmem(w_qkv_shift)), held, len(first),
     )
     from_north = _rows(south, -1)
     from_south = _rows(north, 1)
     query, kv, side_a, side_b, bias = _call(
         own_kernel, (north, south, w_qkv), (bias,),
         (
-            f32(PTOKENS, width), f32(PTOKENS, 2 * width), bf16(2 * PQUAD), bf16(2 * PQUAD),
+            f32(TOKENS + 8, width), f32(TOKENS, 2 * width), bf16(HALF), bf16(HALF),
             _vmem(bias),
         ),
         copies=1,
     )
     from_a = _swap(side_a, 0)
     from_b = _swap(side_b, 1)
-    corner_a = _swap(jnp.concatenate([from_north[:PQUAD], from_south[:PQUAD]], axis=0), 0)
-    corner_b = _swap(jnp.concatenate([from_north[PQUAD:], from_south[PQUAD:]], axis=0), 1)
-    context, kv_b = _call(
+    corner_a = _swap(jnp.concatenate([from_north[:QUAD], from_south[:QUAD]], axis=0), 0)
+    corner_b = _swap(jnp.concatenate([from_north[QUAD:], from_south[QUAD:]], axis=0), 1)
+    far = (w_out_shift, gain_mlp, w_up, w_down)
+    after, kv_b, *weights = _call(
         near_kernel,
-        (from_north, from_south, from_a, from_b, corner_a, query, kv, w_qkv, bias), (),
-        (bf16(2 * PQUAD), f32(4 * PQUAD, 2 * width)),
-        (f32(4 * PQUAD, 2 * width), f32(2 * PQUAD, 2 * width)), flops=10**11,
-    )
-    far = (w_out_shift, gain_mlp, w_up, w_down, to_merge, gain_merge, w_merge)
-    held = [_vmem(array) for array in far]
-    held[4] = bf16(TOKENS, PTOKENS)
+        (from_north, from_south, from_a, from_b, corner_a, kept, query, kv, w_qkv, bias), far,
+        (bf16(HALF), f32(TOKENS, 2 * width), *map(_vmem, far)),
+        (f32(TOKENS, 2 * width), f32(HALF, 2 * width)), len(far), flops=10**11,
+    )
     merged = _call(
-        last_kernel, (corner_b, kept, context, query, kv, kv_b, w_qkv, bias), far,
+        last_kernel, (corner_b, kept, after, query, kv, kv_b, w_qkv, bias, *weights),
+        (to_merge, gain_merge, w_merge),
         jax.ShapeDtypeStruct((QUAD // LEV, LEV, 2 * width), jnp.bfloat16),
-        [f32(2 * PQUAD, 2 * width)] + held, len(far),
+        (
+            f32(HALF, 2 * width), bf16(TOKENS, TOKENS), _vmem(gain_merge), _vmem(w_merge),
+        ),
+        3,
     )
     return merged.reshape(WLAT // 2, WLON // 2, LEV, 2 * width)
 

time: 33.9 us -> 32.8 us (0.968)
  the two profiles are of different devices: /device:TPU:8 before, /device:TPU:6 now
where the time goes in v4:
time: 32.8 us; the launch traced here: 32.6 us
  starting transfers between devices  16.6 us (51%)
  Pallas kernels  15.7 us (48%)
    pallas_call x4, Pallas kernels, _call(): pl.pallas_call(kernel, out_shape=outs, in_specs=[near_spec] * len(near) +...  15.7 us
    ppermute x4, starting transfers between devices, _swap(): return lax.ppermute(value, 'lon', pairs + [(b, a) for a, b in pairs])  14.5 us
    ppermute x2, starting transfers between devices, _rows(): lax.ppermute(value, 'lat', [((i + step) % count, i) for i in range(count)])  2.1 us
  transfers between devices with their start and end apart: 6, of which 0 were waited for; matrix products, arithmetic and copies ran while one was open for 0% of the time, Pallas kernels for 14%

profile of v4, /device:TPU:6, one launch (start us, length us, event | category | flops | bytes accessed | tf_op | source)
XLA Modules:
  0.0 32.6 jit_solution(1869938508304488352)
XLA Ops:
  0.0 4.5 %shard_map.154 = (bf16[288,512]{1,0:T(8,128)(2,1)S(1)}, bf16[144,512]{1,0:T(8,128)(2,1)S(1)}, bf16[144,512]{1,0:T(8,128)(2,1)S(1)}, bf16[512,1536]{1,0:T(8,128)(2,1)S(1)}) custom-call(bf16[72,4,512]{2,1,0:T(4,128)(2,1)} %bitcast.6, bf16[288,288]{1,0:T(8,128)(2,1)} %constant.8.clone.to_win_hbm, f32[1,512]{1,0:T(1,128)} %bitcast.8, ...), custom_call_target="tpu_custom_call" | custom-call | tf_op jit(solution)/shard_map/pallas_call | solution.py:324
  4.5 1.6 %collective-permute-start = (bf16[144,512]{1,0:T(8,128)(2,1)S(1)}, bf16[144,512]{1,0:T(8,128)(2,1)S(1)}, u32[]{:S(2)}, u32[]{:S(2)}) collective-permute-start(bf16[144,512]{1,0:T(8,128)(2,1)S(1)} %get-tuple-element.20.south_ref), channel_id=1, source_target_pairs={{224,0},{0,32},{32,64},{64,96},{96,128},{128,160},{160,192},{192,2... | collective-permute-start | bytes 442376 | tf_op jit(solution)/shard_map/ppermute | solution.py:341
  6.1 0.5 %collective-permute-start.1 = (bf16[144,512]{1,0:T(8,128)(2,1)S(1)}, bf16[144,512]{1,0:T(8,128)(2,1)S(1)}, u32[]{:S(2)}, u32[]{:S(2)}) collective-permute-start(bf16[144,512]{1,0:T(8,128)(2,1)S(1)} %get-tuple-element.21.north_ref), channel_id=1, source_target_pairs={{32,0},{64,32},{96,64},{128,96},{160,128},{192,160},{224,192},{0,2... | collective-permute-start | bytes 442376 | tf_op jit(solution)/shard_map/ppermute | solution.py:341
  6.6 1.0 %shard_map.155 = (f32[296,512]{1,0:T(8,128)S(1)}, f32[288,1024]{1,0:T(8,128)S(1)}, bf16[144,512]{1,0:T(8,128)(2,1)S(1)}, bf16[144,512]{1,0:T(8,128)(2,1)S(1)}, f32[144,320]{1,0:T(8,128)S(1)}) custom-call(bf16[144,512]{1,0:T(8,128)(2,1)S(1)} %get-tuple-element.21.north_ref, bf16[144,512]{1,0:T(8,128)(2,1)S(1)} %get-tuple-element.20.south_ref, ...), custom_call_target="tpu_custom_call" | custom-call | tf_op jit(solution)/shard_map/pallas_call | solution.py:324
  7.6 0.1 collective-permute-start.3
  7.7 8.6 %collective-permute-start.4 = (bf16[144,512]{1,0:T(8,128)(2,1)S(1)}, bf16[144,512]{1,0:T(8,128)(2,1)S(1)}, u32[]{:S(2)}, u32[]{:S(2)}) collective-permute-start(bf16[144,512]{1,0:T(8,128)(2,1)S(1)} %get-tuple-element.25), channel_id=1, source_target_pairs={{1,2},{3,4},{5,6},{7,8},{9,10},{11,12},{13,14},{15,16},{17,18},{19... | collective-permute-start | bytes 442376 | tf_op jit(solution)/shard_map/ppermute | solution.py:347
  16.2 0.0 collective-permute-done.north_ref
  16.3 0.0 collective-permute-done.1.south_ref
  16.3 0.1 collective-permute-start.5
  16.4 5.7 %collective-permute-start.2 = (bf16[144,512]{1,0:T(8,128)(2,1)S(1)}, bf16[144,512]{1,0:T(8,128)(2,1)S(1)}, u32[]{:S(2)}, u32[]{:S(2)}) collective-permute-start(bf16[144,512]{1,0:T(8,128)(2,1)S(1)} %pad_maximum_fusion), channel_id=1, source_target_pairs={{1,2},{3,4},{5,6},{7,8},{9,10},{11,12},{13,14},{15,16},{17,18},{19... | collective-permute-start | bytes 442376 | tf_op jit(solution)/shard_map/ppermute | solution.py:347
  22.2 0.0 collective-permute-done.3.side_a_ref
  22.2 0.0 collective-permute-done.4.side_b_ref
  22.2 0.0 collective-permute-done.5.corner_ref
  22.2 3.8 %shard_map.156 = (bf16[144,512]{1,0:T(8,128)(2,1)S(1)}, f32[288,1024]{1,0:T(8,128)S(1)}, bf16[512,512]{1,0:T(8,128)(2,1)S(1)}, f32[1,512]{1,0:T(1,128)S(1)}, bf1...) custom-call(bf16[144,512]{1,0:T(8,128)(2,1)S(1)} %collective-permute-done.north_ref, ...), custom_call_target="tpu_custom_call" | custom-call | flops 99999997952 | tf_op jit(solution)/shard_map/pallas_call | solution.py:324
  26.0 0.0 collective-permute-done.2.corner_ref
  26.0 6.5 %shard_map.157 = bf16[18,4,1024]{2,1,0:T(4,128)(2,1)} custom-call(bf16[144,512]{1,0:T(8,128)(2,1)S(1)} %collective-permute-done.2.corner_ref, bf16[288,512]{1,0:T(8,128)(2,1)S(1)} %get-tuple-element.22.kept_ref, bf16[144,512]{1,0:T(8,128)(2,1)S(1)} %get-tuple-element.29.after_ref, f32[296,512]{1,0:T(8,128)S(1)} %get-tuple-element.26.query_ref, ...), custom_call_target="tpu_custom_call" | custom-call | tf_op jit(solution)/shard_map/pallas_call | solution.py:324
  (4 shorter events, 0.0 us)
Async XLA Ops:
  4.5 11.8 %collective-permute-start = (bf16[144,512]{1,0:T(8,128)(2,1)S(1)}, bf16[144,512]{1,0:T(8,128)(2,1)S(1)}, u32[]{:S(2)}, u32[]{:S(2)}) collective-permute-start(bf16[144,512]{1,0:T(8,128)(2,1)S(1)} %get-tuple-element.20.south_ref), channel_id=1, source_target_pairs={{224,0},{0,32},{32,64},{64,96},{96,128},{128,160},{160,192},{192,2... | collective-permute-start | bytes 442376 | tf_op jit(solution)/shard_map/ppermute | solution.py:341
  6.1 10.2 %collective-permute-start.1 = (bf16[144,512]{1,0:T(8,128)(2,1)S(1)}, bf16[144,512]{1,0:T(8,128)(2,1)S(1)}, u32[]{:S(2)}, u32[]{:S(2)}) collective-permute-start(bf16[144,512]{1,0:T(8,128)(2,1)S(1)} %get-tuple-element.21.north_ref), channel_id=1, source_target_pairs={{32,0},{64,32},{96,64},{128,96},{160,128},{192,160},{224,192},{0,2... | collective-permute-start | bytes 442376 | tf_op jit(solution)/shard_map/ppermute | solution.py:341
  7.6 14.6 %collective-permute-start.3 = (bf16[144,512]{1,0:T(8,128)(2,1)S(1)}, bf16[144,512]{1,0:T(8,128)(2,1)S(1)}, u32[]{:S(2)}, u32[]{:S(2)}) collective-permute-start(bf16[144,512]{1,0:T(8,128)(2,1)S(1)} %get-tuple-element.24), channel_id=1, source_target_pairs={{0,1},{2,3},{4,5},{6,7},{8,9},{10,11},{12,13},{14,15},{16,17},{18,... | collective-permute-start | bytes 442376 | tf_op jit(solution)/shard_map/ppermute | solution.py:347
  7.7 14.5 %collective-permute-start.4 = (bf16[144,512]{1,0:T(8,128)(2,1)S(1)}, bf16[144,512]{1,0:T(8,128)(2,1)S(1)}, u32[]{:S(2)}, u32[]{:S(2)}) collective-permute-start(bf16[144,512]{1,0:T(8,128)(2,1)S(1)} %get-tuple-element.25), channel_id=1, source_target_pairs={{1,2},{3,4},{5,6},{7,8},{9,10},{11,12},{13,14},{15,16},{17,18},{19... | collective-permute-start | bytes 442376 | tf_op jit(solution)/shard_map/ppermute | solution.py:347
  16.3 5.9 %collective-permute-start.5 = (bf16[144,512]{1,0:T(8,128)(2,1)S(1)}, bf16[144,512]{1,0:T(8,128)(2,1)S(1)}, u32[]{:S(2)}, u32[]{:S(2)}) collective-permute-start(bf16[144,512]{1,0:T(8,128)(2,1)S(1)} %pad_maximum_fusion.1), channel_id=1, source_target_pairs={{0,1},{2,3},{4,5},{6,7},{8,9},{10,11},{12,13},{14,15},{16,17},{18,... | collective-permute-start | bytes 442376 | tf_op jit(solution)/shard_map/ppermute | solution.py:347
  16.4 9.5 %collective-permute-start.2 = (bf16[144,512]{1,0:T(8,128)(2,1)S(1)}, bf16[144,512]{1,0:T(8,128)(2,1)S(1)}, u32[]{:S(2)}, u32[]{:S(2)}) collective-permute-start(bf16[144,512]{1,0:T(8,128)(2,1)S(1)} %pad_maximum_fusion), channel_id=1, source_target_pairs={{1,2},{3,4},{5,6},{7,8},{9,10},{11,12},{13,14},{15,16},{17,18},{19... | collective-permute-start | bytes 442376 | tf_op jit(solution)/shard_map/ppermute | solution.py:347

commit v5 on v4

--- a/solution.py
+++ b/solution.py
@@ -134,6 +134,10 @@
     ).astype(jnp.bfloat16)
 
 
+def stage(body):
+    pl.when(lax.axis_index("lat") >= 0)(body)
+
+
 def halves(ref):
     values = ref[...].astype(jnp.float32)
     return values[:QUAD], values[QUAD:]
@@ -258,7 +262,7 @@
     north_ref, south_ref, side_a_ref, side_b_ref, corner_ref, kept_ref, query_ref, kv_ref,
     w_qkv_ref, bias_ref, w_out_hbm, gain_mlp_hbm, w_up_hbm, w_down_hbm,
     after_ref, kv_b_ref, w_out_ref, gain_mlp_ref, w_up_ref, w_down_ref,
-    kv_a_ref, kv_corner_ref, sems,
+    kv_a_ref, kv_corner_ref, context_ref, sems,
 ):
     pairs = (
         (w_out_hbm, w_out_ref), (gain_mlp_hbm, gain_mlp_ref), (w_up_hbm, w_up_ref),
@@ -274,21 +278,28 @@
         return array
 
     width = query_ref.shape[-1]
-    w_kv = w_qkv_ref[:, width:]
-    (north_a, north_b), (south_a, south_b) = halves(north_ref), halves(south_ref)
-    kv_a_ref[:HALF] = dot(rounded(north_a, south_a), w_kv)
-    kv_a_ref[HALF:] = dot(side_a_ref[...], w_kv)
-    kv_corner_ref[...] = dot(corner_ref[...], w_kv)
-    kv_b_ref[:HALF] = dot(rounded(north_b, south_b), w_kv)
-    kv_b_ref[HALF:] = dot(side_b_ref[...], w_kv)
-    context = side_context(0, query_ref, kv_ref, kv_a_ref, kv_corner_ref, bias_ref)
-    after_ref[...] = block(context, kept_ref[:HALF], *map(arrived, range(4)))
+
+    @stage
+    def _():
+        (north_a, north_b), (south_a, south_b) = halves(north_ref), halves(south_ref)
+        w_kv = w_qkv_ref[:, width:]
+        kv_a_ref[:HALF] = dot(rounded(north_a, south_a), w_kv)
+        kv_a_ref[HALF:] = dot(side_a_ref[...], w_kv)
+        kv_corner_ref[...] = dot(corner_ref[...], w_kv)
+        kv_b_ref[:HALF] = dot(rounded(north_b, south_b), w_kv)
+        kv_b_ref[HALF:] = dot(side_b_ref[...], w_kv)
+
+    @stage
+    def _():
+        context_ref[...] = side_context(0, query_ref, kv_ref, kv_a_ref, kv_corner_ref, bias_ref)
+
+    after_ref[...] = block(context_ref[...], kept_ref[:HALF], *map(arrived, range(4)))
 
 
 def last_kernel(
     corner_ref, kept_ref, after_ref, query_ref, kv_ref, kv_b_ref, w_qkv_ref, bias_ref,
     w_out_ref, gain_mlp_ref, w_up_ref, w_down_ref, to_merge_hbm, gain_merge_hbm, w_merge_hbm,
-    out_ref, kv_corner_ref, to_merge_ref, gain_merge_ref, w_merge_ref, sems,
+    out_ref, kv_corner_ref, context_ref, to_merge_ref, gain_merge_ref, w_merge_ref, sems,
 ):
     odd = lax.rem(lax.axis_index("lon"), 2)
     copies = _fetch(
@@ -299,11 +310,18 @@
         sems,
     )
     width = kept_ref.shape[-1]
-    kv_corner_ref[...] = dot(corner_ref[...], w_qkv_ref[:, width:])
-    context = side_context(1, query_ref, kv_ref, kv_b_ref, kv_corner_ref, bias_ref)
+
+    @stage
+    def _():
+        kv_corner_ref[...] = dot(corner_ref[...], w_qkv_ref[:, width:])
+
+    @stage
+    def _():
+        context_ref[...] = side_context(1, query_ref, kv_ref, kv_b_ref, kv_corner_ref, bias_ref)
+
     weights = (w_out_ref, gain_mlp_ref, w_up_ref, w_down_ref)
     after = block(
-        context, kept_ref[HALF:], *(lambda ref=ref: ref[...] for ref in weights)
+        context_ref[...], kept_ref[HALF:], *(lambda ref=ref: ref[...] for ref in weights)
     )
     copies[0].wait()
     merge = dot(to_merge_ref[...], jnp.concatenate([after_ref[...], after], axis=0))
@@ -395,14 +413,14 @@
         near_kernel,
         (from_north, from_south, from_a, from_b, corner_a, kept, query, kv, w_qkv, bias), far,
         (bf16(HALF), f32(TOKENS, 2 * width), *map(_vmem, far)),
-        (f32(TOKENS, 2 * width), f32(HALF, 2 * width)), len(far), flops=10**11,
+        (f32(TOKENS, 2 * width), f32(HALF, 2 * width), bf16(HALF)), len(far), flops=10**11,
     )
     merged = _call(
         last_kernel, (corner_b, kept, after, query, kv, kv_b, w_qkv, bias, *weights),
         (to_merge, gain_merge, w_merge),
         jax.ShapeDtypeStruct((QUAD // LEV, LEV, 2 * width), jnp.bfloat16),
         (
-            f32(HALF, 2 * width), bf16(TOKENS, TOKENS), _vmem(gain_merge), _vmem(w_merge),
+            f32(HALF, 2 * width), bf16(HALF), bf16(TOKENS, TOKENS), _vmem(gain_merge), _vmem(w_merge),
         ),
         3,
     )

time: 32.8 us -> 31 us (0.945)
  Pallas kernels: 15.7 us -> 14.2 us
    pallas_call x4, Pallas kernels: 15.7 us -> 14.2 us  [_call(): pl.pallas_call(kernel, out_shape=outs, in_specs=[near_spec] * len(near) +...]
  transfers between devices with their start and end apart: 6 -> 6, of which waited for: 0 -> 0; matrix products, arithmetic and copies ran while one was open for 0% -> 0% of each run, Pallas kernels for 14% -> 15%
where the time goes in v5:
time: 31 us; the launch traced here: 30.8 us
  starting transfers between devices  16.4 us (53%)
  Pallas kernels  14.2 us (46%)
    ppermute x4, starting transfers between devices, _swap(): return lax.ppermute(value, 'lon', pairs + [(b, a) for a, b in pairs])  14.3 us
    pallas_call x4, Pallas kernels, _call(): pl.pallas_call(kernel, out_shape=outs, in_specs=[near_spec] * len(near) +...  14.2 us
    ppermute x2, starting transfers between devices, _rows(): lax.ppermute(value, 'lat', [((i + step) % count, i) for i in range(count)])  2.1 us
  transfers between devices with their start and end apart: 6, of which 0 were waited for; matrix products, arithmetic and copies ran while one was open for 0% of the time, Pallas kernels for 15%

profile of v5, /device:TPU:6, one launch (start us, length us, event | category | flops | bytes accessed | tf_op | source)
XLA Modules:
  0.0 30.8 jit_solution(10698685131986518415)
XLA Ops:
  0.0 4.5 %shard_map.154 = (bf16[288,512]{1,0:T(8,128)(2,1)S(1)}, bf16[144,512]{1,0:T(8,128)(2,1)S(1)}, bf16[144,512]{1,0:T(8,128)(2,1)S(1)}, bf16[512,1536]{1,0:T(8,128)(2,1)S(1)}) custom-call(bf16[72,4,512]{2,1,0:T(4,128)(2,1)} %bitcast.6, bf16[288,288]{1,0:T(8,128)(2,1)} %constant.8.clone.to_win_hbm, f32[1,512]{1,0:T(1,128)} %bitcast.8, ...), custom_call_target="tpu_custom_call" | custom-call | tf_op jit(solution)/shard_map/pallas_call | solution.py:342
  4.5 1.6 %collective-permute-start = (bf16[144,512]{1,0:T(8,128)(2,1)S(1)}, bf16[144,512]{1,0:T(8,128)(2,1)S(1)}, u32[]{:S(2)}, u32[]{:S(2)}) collective-permute-start(bf16[144,512]{1,0:T(8,128)(2,1)S(1)} %get-tuple-element.20.south_ref), channel_id=1, source_target_pairs={{224,0},{0,32},{32,64},{64,96},{96,128},{128,160},{160,192},{192,2... | collective-permute-start | bytes 442376 | tf_op jit(solution)/shard_map/ppermute | solution.py:359
  6.1 0.5 %collective-permute-start.1 = (bf16[144,512]{1,0:T(8,128)(2,1)S(1)}, bf16[144,512]{1,0:T(8,128)(2,1)S(1)}, u32[]{:S(2)}, u32[]{:S(2)}) collective-permute-start(bf16[144,512]{1,0:T(8,128)(2,1)S(1)} %get-tuple-element.21.north_ref), channel_id=1, source_target_pairs={{32,0},{64,32},{96,64},{128,96},{160,128},{192,160},{224,192},{0,2... | collective-permute-start | bytes 442376 | tf_op jit(solution)/shard_map/ppermute | solution.py:359
  6.6 1.0 %shard_map.155 = (f32[296,512]{1,0:T(8,128)S(1)}, f32[288,1024]{1,0:T(8,128)S(1)}, bf16[144,512]{1,0:T(8,128)(2,1)S(1)}, bf16[144,512]{1,0:T(8,128)(2,1)S(1)}, f32[144,320]{1,0:T(8,128)S(1)}) custom-call(bf16[144,512]{1,0:T(8,128)(2,1)S(1)} %get-tuple-element.21.north_ref, bf16[144,512]{1,0:T(8,128)(2,1)S(1)} %get-tuple-element.20.south_ref, ...), custom_call_target="tpu_custom_call" | custom-call | tf_op jit(solution)/shard_map/pallas_call | solution.py:342
  7.6 0.1 collective-permute-start.3
  7.7 8.6 %collective-permute-start.4 = (bf16[144,512]{1,0:T(8,128)(2,1)S(1)}, bf16[144,512]{1,0:T(8,128)(2,1)S(1)}, u32[]{:S(2)}, u32[]{:S(2)}) collective-permute-start(bf16[144,512]{1,0:T(8,128)(2,1)S(1)} %get-tuple-element.25), channel_id=1, source_target_pairs={{1,2},{3,4},{5,6},{7,8},{9,10},{11,12},{13,14},{15,16},{17,18},{19... | collective-permute-start | bytes 442376 | tf_op jit(solution)/shard_map/ppermute | solution.py:365
  16.2 0.0 collective-permute-done.north_ref
  16.3 0.0 collective-permute-done.1.south_ref
  16.3 0.1 collective-permute-start.5
  16.4 5.6 %collective-permute-start.2 = (bf16[144,512]{1,0:T(8,128)(2,1)S(1)}, bf16[144,512]{1,0:T(8,128)(2,1)S(1)}, u32[]{:S(2)}, u32[]{:S(2)}) collective-permute-start(bf16[144,512]{1,0:T(8,128)(2,1)S(1)} %pad_maximum_fusion), channel_id=1, source_target_pairs={{1,2},{3,4},{5,6},{7,8},{9,10},{11,12},{13,14},{15,16},{17,18},{19... | collective-permute-start | bytes 442376 | tf_op jit(solution)/shard_map/ppermute | solution.py:365
  22.0 0.0 collective-permute-done.3.side_a_ref
  22.0 0.0 collective-permute-done.4.side_b_ref
  22.0 0.0 collective-permute-done.5.corner_ref
  22.0 3.7 %shard_map.156 = (bf16[144,512]{1,0:T(8,128)(2,1)S(1)}, f32[288,1024]{1,0:T(8,128)S(1)}, bf16[512,512]{1,0:T(8,128)(2,1)S(1)}, f32[1,512]{1,0:T(1,128)S(1)}, bf1...) custom-call(bf16[144,512]{1,0:T(8,128)(2,1)S(1)} %collective-permute-done.north_ref, ...), custom_call_target="tpu_custom_call" | custom-call | flops 99999997952 | tf_op jit(solution)/shard_map/pallas_call | solution.py:342
  25.8 0.0 collective-permute-done.2.corner_ref
  25.8 5.0 %shard_map.157 = bf16[18,4,1024]{2,1,0:T(4,128)(2,1)} custom-call(bf16[144,512]{1,0:T(8,128)(2,1)S(1)} %collective-permute-done.2.corner_ref, bf16[288,512]{1,0:T(8,128)(2,1)S(1)} %get-tuple-element.22.kept_ref, bf16[144,512]{1,0:T(8,128)(2,1)S(1)} %get-tuple-element.29.after_ref, f32[296,512]{1,0:T(8,128)S(1)} %get-tuple-element.26.query_ref, ...), custom_call_target="tpu_custom_call" | custom-call | tf_op jit(solution)/shard_map/pallas_call | solution.py:342
  (4 shorter events, 0.0 us)
Async XLA Ops:
  4.5 11.8 %collective-permute-start = (bf16[144,512]{1,0:T(8,128)(2,1)S(1)}, bf16[144,512]{1,0:T(8,128)(2,1)S(1)}, u32[]{:S(2)}, u32[]{:S(2)}) collective-permute-start(bf16[144,512]{1,0:T(8,128)(2,1)S(1)} %get-tuple-element.20.south_ref), channel_id=1, source_target_pairs={{224,0},{0,32},{32,64},{64,96},{96,128},{128,160},{160,192},{192,2... | collective-permute-start | bytes 442376 | tf_op jit(solution)/shard_map/ppermute | solution.py:359
  6.1 10.2 %collective-permute-start.1 = (bf16[144,512]{1,0:T(8,128)(2,1)S(1)}, bf16[144,512]{1,0:T(8,128)(2,1)S(1)}, u32[]{:S(2)}, u32[]{:S(2)}) collective-permute-start(bf16[144,512]{1,0:T(8,128)(2,1)S(1)} %get-tuple-element.21.north_ref), channel_id=1, source_target_pairs={{32,0},{64,32},{96,64},{128,96},{160,128},{192,160},{224,192},{0,2... | collective-permute-start | bytes 442376 | tf_op jit(solution)/shard_map/ppermute | solution.py:359
  7.6 14.5 %collective-permute-start.3 = (bf16[144,512]{1,0:T(8,128)(2,1)S(1)}, bf16[144,512]{1,0:T(8,128)(2,1)S(1)}, u32[]{:S(2)}, u32[]{:S(2)}) collective-permute-start(bf16[144,512]{1,0:T(8,128)(2,1)S(1)} %get-tuple-element.24), channel_id=1, source_target_pairs={{0,1},{2,3},{4,5},{6,7},{8,9},{10,11},{12,13},{14,15},{16,17},{18,... | collective-permute-start | bytes 442376 | tf_op jit(solution)/shard_map/ppermute | solution.py:365
  7.7 14.4 %collective-permute-start.4 = (bf16[144,512]{1,0:T(8,128)(2,1)S(1)}, bf16[144,512]{1,0:T(8,128)(2,1)S(1)}, u32[]{:S(2)}, u32[]{:S(2)}) collective-permute-start(bf16[144,512]{1,0:T(8,128)(2,1)S(1)} %get-tuple-element.25), channel_id=1, source_target_pairs={{1,2},{3,4},{5,6},{7,8},{9,10},{11,12},{13,14},{15,16},{17,18},{19... | collective-permute-start | bytes 442376 | tf_op jit(solution)/shard_map/ppermute | solution.py:365
  16.3 5.7 %collective-permute-start.5 = (bf16[144,512]{1,0:T(8,128)(2,1)S(1)}, bf16[144,512]{1,0:T(8,128)(2,1)S(1)}, u32[]{:S(2)}, u32[]{:S(2)}) collective-permute-start(bf16[144,512]{1,0:T(8,128)(2,1)S(1)} %pad_maximum_fusion.1), channel_id=1, source_target_pairs={{0,1},{2,3},{4,5},{6,7},{8,9},{10,11},{12,13},{14,15},{16,17},{18,... | collective-permute-start | bytes 442376 | tf_op jit(solution)/shard_map/ppermute | solution.py:365
  16.4 9.3 %collective-permute-start.2 = (bf16[144,512]{1,0:T(8,128)(2,1)S(1)}, bf16[144,512]{1,0:T(8,128)(2,1)S(1)}, u32[]{:S(2)}, u32[]{:S(2)}) collective-permute-start(bf16[144,512]{1,0:T(8,128)(2,1)S(1)} %pad_maximum_fusion), channel_id=1, source_target_pairs={{1,2},{3,4},{5,6},{7,8},{9,10},{11,12},{13,14},{15,16},{17,18},{19... | collective-permute-start | bytes 442376 | tf_op jit(solution)/shard_map/ppermute | solution.py:365

commit v6 on v5

--- a/solution.py
+++ b/solution.py
@@ -159,7 +159,7 @@
 
 def window_kernel(
     x_hbm, to_win_hbm, gain_hbm, w_qkv_hbm, w_out_hbm, to_quad_hbm, gain_shift_hbm,
-    w_next_hbm, kept_ref, north_ref, south_ref, w_next_ref,
+    w_next_hbm, bias_hbm, kept_ref, north_ref, south_ref, w_next_ref, bias_ref,
     x_ref, to_win_ref, gain_ref, w_qkv_ref, w_out_ref, to_quad_ref, gain_shift_ref, sems,
 ):
     odd = lax.rem(lax.axis_index("lon"), 2)
@@ -168,7 +168,7 @@
             (x_hbm, x_ref), (to_win_hbm, to_win_ref), (gain_hbm, gain_ref),
             (w_qkv_hbm, w_qkv_ref), (w_out_hbm, w_out_ref),
             (to_quad_hbm.at[odd], to_quad_ref), (gain_shift_hbm, gain_shift_ref),
-            (w_next_hbm, w_next_ref),
+            (w_next_hbm, w_next_ref), (bias_hbm, bias_ref),
         ),
         sems,
     )
@@ -201,13 +201,12 @@
             *(quads[start : start + QUAD] for start in (half * QUAD, HALF + half * QUAD))
         )
     copies[7].wait()
+    copies[8].wait()
 
 
 def own_kernel(
-    north_ref, south_ref, w_qkv_ref, bias_hbm,
-    query_ref, kv_ref, side_a_ref, side_b_ref, bias_ref, sems,
+    north_ref, south_ref, w_qkv_ref, query_ref, kv_ref, side_a_ref, side_b_ref
 ):
-    copies = _fetch(((bias_hbm, bias_ref),), sems)
     (na, nb), (sa, sb) = halves(north_ref), halves(south_ref)
     side_a, side_b = rounded(na, sa), rounded(nb, sb)
     side_a_ref[...] = side_a
@@ -217,7 +216,6 @@
     query_ref[:TOKENS] = dot(tokens, w_qkv_ref[:, :width])
     query_ref[TOKENS:] = jnp.zeros_like(query_ref[TOKENS:])
     kv_ref[...] = dot(tokens, w_qkv_ref[:, width:])
-    copies[0].wait()
 
 
 def side_context(side, query_ref, kv_ref, kv_near_ref, kv_corner_ref, bias_ref):
@@ -282,12 +280,17 @@
     @stage
     def _():
         (north_a, north_b), (south_a, south_b) = halves(north_ref), halves(south_ref)
-        w_kv = w_qkv_ref[:, width:]
-        kv_a_ref[:HALF] = dot(rounded(north_a, south_a), w_kv)
-        kv_a_ref[HALF:] = dot(side_a_ref[...], w_kv)
-        kv_corner_ref[...] = dot(corner_ref[...], w_kv)
-        kv_b_ref[:HALF] = dot(rounded(north_b, south_b), w_kv)
-        kv_b_ref[HALF:] = dot(side_b_ref[...], w_kv)
+        tokens = jnp.concatenate(
+            [
+                rounded(north_a, south_a), side_a_ref[...], corner_ref[...],
+                rounded(north_b, south_b), side_b_ref[...],
+            ],
+            axis=0,
+        )
+        halo = dot(tokens, w_qkv_ref[:, width:])
+        kv_a_ref[...] = halo[:TOKENS]
+        kv_corner_ref[...] = halo[TOKENS : TOKENS + HALF]
+        kv_b_ref[...] = halo[TOKENS + HALF :]
 
     @stage
     def _():
@@ -387,22 +390,18 @@
         return pltpu.VMEM((rows, cols), jnp.float32)
 
     x = latent_field.reshape(WLAT * WLON, LEV, width)
-    first = (x, to_win, gain_win, w_qkv_win, w_out_win, to_quad, gain_shift, w_qkv_shift)
-    held = [_vmem(array) for array in first[:-1]]
+    first = (x, to_win, gain_win, w_qkv_win, w_out_win, to_quad, gain_shift, w_qkv_shift, bias)
+    held = [_vmem(array) for array in first[:-2]]
     held[5] = bf16(TOKENS, TOKENS)
-    kept, north, south, w_qkv = _call(
+    kept, north, south, w_qkv, bias = _call(
         window_kernel, (), first,
-        (bf16(TOKENS), bf16(HALF), bf16(HALF), _vmem(w_qkv_shift)), held, len(first),
+        (bf16(TOKENS), bf16(HALF), bf16(HALF), _vmem(w_qkv_shift), _vmem(bias)), held, len(first),
     )
     from_north = _rows(south, -1)
     from_south = _rows(north, 1)
-    query, kv, side_a, side_b, bias = _call(
-        own_kernel, (north, south, w_qkv), (bias,),
-        (
-            f32(TOKENS + 8, width), f32(TOKENS, 2 * width), bf16(HALF), bf16(HALF),
-            _vmem(bias),
-        ),
-        copies=1,
+    query, kv, side_a, side_b = _call(
+        own_kernel, (north, south, w_qkv), (),
+        (f32(TOKENS + 8, width), f32(TOKENS, 2 * width), bf16(HALF), bf16(HALF)),
     )
     from_a = _swap(side_a, 0)
     from_b = _swap(side_b, 1)

time: 31 us -> 30.9 us (level)
  starting transfers between devices: 16.4 us -> 16.8 us
    ppermute x4, starting transfers between devices: 14.3 us -> 14.7 us  [_swap(): return lax.ppermute(value, 'lon', pairs + [(b, a) for a, b in pairs])]
    pallas_call x4, Pallas kernels: 14.2 us -> 13.9 us  [_call(): pl.pallas_call(kernel, out_shape=outs, in_specs=[near_spec] * len(near) +...]
  transfers between devices with their start and end apart: 6 -> 6, of which waited for: 0 -> 0; matrix products, arithmetic and copies ran while one was open for 0% -> 0% of each run, Pallas kernels for 15% -> 14%
where the time goes in v6:
time: 30.9 us; the launch traced here: 30.8 us
  starting transfers between devices  16.8 us (54%)
  Pallas kernels  13.9 us (45%)
    ppermute x4, starting transfers between devices, _swap(): return lax.ppermute(value, 'lon', pairs + [(b, a) for a, b in pairs])  14.7 us
    pallas_call x4, Pallas kernels, _call(): pl.pallas_call(kernel, out_shape=outs, in_specs=[near_spec] * len(near) +...  13.9 us
    ppermute x2, starting transfers between devices, _rows(): lax.ppermute(value, 'lat', [((i + step) % count, i) for i in range(count)])  2.1 us
  transfers between devices with their start and end apart: 6, of which 0 were waited for; matrix products, arithmetic and copies ran while one was open for 0% of the time, Pallas kernels for 14%

profile of v6, /device:TPU:6, one launch (start us, length us, event | category | flops | bytes accessed | tf_op | source)
XLA Modules:
  0.0 30.8 jit_solution(15824241149563620185)
XLA Ops:
  0.0 4.5 %shard_map.154 = (bf16[288,512]{1,0:T(8,128)(2,1)S(1)}, bf16[144,512]{1,0:T(8,128)(2,1)S(1)}, bf16[144,512]{1,0:T(8,128)(2,1)S(1)}, bf16[512,1536]{1,0:T(8,128)(2,1)S(1)}, f32[144,320]{1,0:T(8,128)S(1)}) custom-call(bf16[72,4,512]{2,1,0:T(4,128)(2,1)} %bitcast.6, bf16[288,288]{1,0:T(8,128)(2,1)} %constant.8.clone.to_win_hbm, f32[1,512]{1,0:T(1,128)} %bitcast.8, ...), custom_call_target="tpu_custom_call" | custom-call | tf_op jit(solution)/shard_map/pallas_call | solution.py:345
  4.5 1.6 %collective-permute-start = (bf16[144,512]{1,0:T(8,128)(2,1)S(1)}, bf16[144,512]{1,0:T(8,128)(2,1)S(1)}, u32[]{:S(2)}, u32[]{:S(2)}) collective-permute-start(bf16[144,512]{1,0:T(8,128)(2,1)S(1)} %get-tuple-element.20.south_ref), channel_id=1, source_target_pairs={{224,0},{0,32},{32,64},{64,96},{96,128},{128,160},{160,192},{192,2... | collective-permute-start | bytes 442376 | tf_op jit(solution)/shard_map/ppermute | solution.py:362
  6.1 0.5 %collective-permute-start.1 = (bf16[144,512]{1,0:T(8,128)(2,1)S(1)}, bf16[144,512]{1,0:T(8,128)(2,1)S(1)}, u32[]{:S(2)}, u32[]{:S(2)}) collective-permute-start(bf16[144,512]{1,0:T(8,128)(2,1)S(1)} %get-tuple-element.21.north_ref), channel_id=1, source_target_pairs={{32,0},{64,32},{96,64},{128,96},{160,128},{192,160},{224,192},{0,2... | collective-permute-start | bytes 442376 | tf_op jit(solution)/shard_map/ppermute | solution.py:362
  6.6 0.6 %shard_map.155 = (f32[296,512]{1,0:T(8,128)S(1)}, f32[288,1024]{1,0:T(8,128)S(1)}, bf16[144,512]{1,0:T(8,128)(2,1)S(1)}, bf16[144,512]{1,0:T(8,128)(2,1)S(1)}) custom-call(bf16[144,512]{1,0:T(8,128)(2,1)S(1)} %get-tuple-element.21.north_ref, bf16[144,512]{1,0:T(8,128)(2,1)S(1)} %get-tuple-element.20.south_ref, bf16[512,1536]{1,0:T(8,128)(2,1)S(1)} %get-tuple-element.23.w_qkv_ref), custom_call_target="tpu_custom_call" | custom-call | tf_op jit(solution)/shard_map/pallas_call | solution.py:345
  7.2 0.1 collective-permute-start.3
  7.3 8.6 %collective-permute-start.4 = (bf16[144,512]{1,0:T(8,128)(2,1)S(1)}, bf16[144,512]{1,0:T(8,128)(2,1)S(1)}, u32[]{:S(2)}, u32[]{:S(2)}) collective-permute-start(bf16[144,512]{1,0:T(8,128)(2,1)S(1)} %get-tuple-element.25), channel_id=1, source_target_pairs={{1,2},{3,4},{5,6},{7,8},{9,10},{11,12},{13,14},{15,16},{17,18},{19... | collective-permute-start | bytes 442376 | tf_op jit(solution)/shard_map/ppermute | solution.py:368
  15.9 0.0 collective-permute-done.north_ref
  15.9 0.0 collective-permute-done.1.south_ref
  16.0 0.1 collective-permute-start.5
  16.1 5.9 %collective-permute-start.2 = (bf16[144,512]{1,0:T(8,128)(2,1)S(1)}, bf16[144,512]{1,0:T(8,128)(2,1)S(1)}, u32[]{:S(2)}, u32[]{:S(2)}) collective-permute-start(bf16[144,512]{1,0:T(8,128)(2,1)S(1)} %pad_maximum_fusion), channel_id=1, source_target_pairs={{1,2},{3,4},{5,6},{7,8},{9,10},{11,12},{13,14},{15,16},{17,18},{19... | collective-permute-start | bytes 442376 | tf_op jit(solution)/shard_map/ppermute | solution.py:368
  22.0 0.0 collective-permute-done.3.side_a_ref
  22.0 0.0 collective-permute-done.4.side_b_ref
  22.0 0.0 collective-permute-done.5.corner_ref
  22.0 3.7 %shard_map.156 = (bf16[144,512]{1,0:T(8,128)(2,1)S(1)}, f32[288,1024]{1,0:T(8,128)S(1)}, bf16[512,512]{1,0:T(8,128)(2,1)S(1)}, f32[1,512]{1,0:T(1,128)S(1)}, bf1...) custom-call(bf16[144,512]{1,0:T(8,128)(2,1)S(1)} %collective-permute-done.north_ref, ...), custom_call_target="tpu_custom_call" | custom-call | flops 99999997952 | tf_op jit(solution)/shard_map/pallas_call | solution.py:345
  25.7 0.0 collective-permute-done.2.corner_ref
  25.8 5.1 %shard_map.157 = bf16[18,4,1024]{2,1,0:T(4,128)(2,1)} custom-call(bf16[144,512]{1,0:T(8,128)(2,1)S(1)} %collective-permute-done.2.corner_ref, bf16[288,512]{1,0:T(8,128)(2,1)S(1)} %get-tuple-element.22.kept_ref, bf16[144,512]{1,0:T(8,128)(2,1)S(1)} %get-tuple-element.29.after_ref, f32[296,512]{1,0:T(8,128)S(1)} %get-tuple-element.26.query_ref, ...), custom_call_target="tpu_custom_call" | custom-call | tf_op jit(solution)/shard_map/pallas_call | solution.py:345
  (4 shorter events, 0.0 us)
Async XLA Ops:
  4.5 11.4 %collective-permute-start = (bf16[144,512]{1,0:T(8,128)(2,1)S(1)}, bf16[144,512]{1,0:T(8,128)(2,1)S(1)}, u32[]{:S(2)}, u32[]{:S(2)}) collective-permute-start(bf16[144,512]{1,0:T(8,128)(2,1)S(1)} %get-tuple-element.20.south_ref), channel_id=1, source_target_pairs={{224,0},{0,32},{32,64},{64,96},{96,128},{128,160},{160,192},{192,2... | collective-permute-start | bytes 442376 | tf_op jit(solution)/shard_map/ppermute | solution.py:362
  6.1 9.9 %collective-permute-start.1 = (bf16[144,512]{1,0:T(8,128)(2,1)S(1)}, bf16[144,512]{1,0:T(8,128)(2,1)S(1)}, u32[]{:S(2)}, u32[]{:S(2)}) collective-permute-start(bf16[144,512]{1,0:T(8,128)(2,1)S(1)} %get-tuple-element.21.north_ref), channel_id=1, source_target_pairs={{32,0},{64,32},{96,64},{128,96},{160,128},{192,160},{224,192},{0,2... | collective-permute-start | bytes 442376 | tf_op jit(solution)/shard_map/ppermute | solution.py:362
  7.2 14.8 %collective-permute-start.3 = (bf16[144,512]{1,0:T(8,128)(2,1)S(1)}, bf16[144,512]{1,0:T(8,128)(2,1)S(1)}, u32[]{:S(2)}, u32[]{:S(2)}) collective-permute-start(bf16[144,512]{1,0:T(8,128)(2,1)S(1)} %get-tuple-element.24), channel_id=1, source_target_pairs={{0,1},{2,3},{4,5},{6,7},{8,9},{10,11},{12,13},{14,15},{16,17},{18,... | collective-permute-start | bytes 442376 | tf_op jit(solution)/shard_map/ppermute | solution.py:368
  7.3 14.7 %collective-permute-start.4 = (bf16[144,512]{1,0:T(8,128)(2,1)S(1)}, bf16[144,512]{1,0:T(8,128)(2,1)S(1)}, u32[]{:S(2)}, u32[]{:S(2)}) collective-permute-start(bf16[144,512]{1,0:T(8,128)(2,1)S(1)} %get-tuple-element.25), channel_id=1, source_target_pairs={{1,2},{3,4},{5,6},{7,8},{9,10},{11,12},{13,14},{15,16},{17,18},{19... | collective-permute-start | bytes 442376 | tf_op jit(solution)/shard_map/ppermute | solution.py:368
  16.0 6.0 %collective-permute-start.5 = (bf16[144,512]{1,0:T(8,128)(2,1)S(1)}, bf16[144,512]{1,0:T(8,128)(2,1)S(1)}, u32[]{:S(2)}, u32[]{:S(2)}) collective-permute-start(bf16[144,512]{1,0:T(8,128)(2,1)S(1)} %pad_maximum_fusion.1), channel_id=1, source_target_pairs={{0,1},{2,3},{4,5},{6,7},{8,9},{10,11},{12,13},{14,15},{16,17},{18,... | collective-permute-start | bytes 442376 | tf_op jit(solution)/shard_map/ppermute | solution.py:368
  16.1 9.6 %collective-permute-start.2 = (bf16[144,512]{1,0:T(8,128)(2,1)S(1)}, bf16[144,512]{1,0:T(8,128)(2,1)S(1)}, u32[]{:S(2)}, u32[]{:S(2)}) collective-permute-start(bf16[144,512]{1,0:T(8,128)(2,1)S(1)} %pad_maximum_fusion), channel_id=1, source_target_pairs={{1,2},{3,4},{5,6},{7,8},{9,10},{11,12},{13,14},{15,16},{17,18},{19... | collective-permute-start | bytes 442376 | tf_op jit(solution)/shard_map/ppermute | solution.py:368

commit v7 on v6

--- a/solution.py
+++ b/solution.py
@@ -172,11 +172,12 @@
         ),
         sems,
     )
-    for copy in copies[:3]:
-        copy.wait()
+    copies[0].wait()
     width = x_ref.shape[-1]
     x = x_ref[...].astype(jnp.float32).reshape(TOKENS, width).astype(jnp.bfloat16)
+    copies[1].wait()
     x = dot(to_win_ref[...], x)
+    copies[2].wait()
     tokens = normed(x, gain_ref[...]).astype(jnp.bfloat16)
     copies[3].wait()
     query, key, value = (

time: 30.9 us -> 30.9 us (level)
  no operation moved by 1% of the time
where the time goes in v7:
time: 30.9 us; the launch traced here: 30.8 us
  starting transfers between devices  16.8 us (54%)
  Pallas kernels  13.9 us (45%)
    ppermute x4, starting transfers between devices, _swap(): return lax.ppermute(value, 'lon', pairs + [(b, a) for a, b in pairs])  14.7 us
    pallas_call x4, Pallas kernels, _call(): pl.pallas_call(kernel, out_shape=outs, in_specs=[near_spec] * len(near) +...  13.9 us
    ppermute x2, starting transfers between devices, _rows(): lax.ppermute(value, 'lat', [((i + step) % count, i) for i in range(count)])  2.1 us
  transfers between devices with their start and end apart: 6, of which 0 were waited for; matrix products, arithmetic and copies ran while one was open for 0% of the time, Pallas kernels for 14%

profile of v7, /device:TPU:6, one launch (start us, length us, event | category | flops | bytes accessed | tf_op | source)
XLA Modules:
  0.0 30.8 jit_solution(1069919236476005565)
XLA Ops:
  0.0 4.5 %shard_map.154 = (bf16[288,512]{1,0:T(8,128)(2,1)S(1)}, bf16[144,512]{1,0:T(8,128)(2,1)S(1)}, bf16[144,512]{1,0:T(8,128)(2,1)S(1)}, bf16[512,1536]{1,0:T(8,128)(2,1)S(1)}, f32[144,320]{1,0:T(8,128)S(1)}) custom-call(bf16[72,4,512]{2,1,0:T(4,128)(2,1)} %bitcast.6, bf16[288,288]{1,0:T(8,128)(2,1)} %constant.8.clone.to_win_hbm, f32[1,512]{1,0:T(1,128)} %bitcast.8, ...), custom_call_target="tpu_custom_call" | custom-call | tf_op jit(solution)/shard_map/pallas_call | solution.py:346
  4.5 1.6 %collective-permute-start = (bf16[144,512]{1,0:T(8,128)(2,1)S(1)}, bf16[144,512]{1,0:T(8,128)(2,1)S(1)}, u32[]{:S(2)}, u32[]{:S(2)}) collective-permute-start(bf16[144,512]{1,0:T(8,128)(2,1)S(1)} %get-tuple-element.20.south_ref), channel_id=1, source_target_pairs={{224,0},{0,32},{32,64},{64,96},{96,128},{128,160},{160,192},{192,2... | collective-permute-start | bytes 442376 | tf_op jit(solution)/shard_map/ppermute | solution.py:363
  6.1 0.5 %collective-permute-start.1 = (bf16[144,512]{1,0:T(8,128)(2,1)S(1)}, bf16[144,512]{1,0:T(8,128)(2,1)S(1)}, u32[]{:S(2)}, u32[]{:S(2)}) collective-permute-start(bf16[144,512]{1,0:T(8,128)(2,1)S(1)} %get-tuple-element.21.north_ref), channel_id=1, source_target_pairs={{32,0},{64,32},{96,64},{128,96},{160,128},{192,160},{224,192},{0,2... | collective-permute-start | bytes 442376 | tf_op jit(solution)/shard_map/ppermute | solution.py:363
  6.6 0.6 %shard_map.155 = (f32[296,512]{1,0:T(8,128)S(1)}, f32[288,1024]{1,0:T(8,128)S(1)}, bf16[144,512]{1,0:T(8,128)(2,1)S(1)}, bf16[144,512]{1,0:T(8,128)(2,1)S(1)}) custom-call(bf16[144,512]{1,0:T(8,128)(2,1)S(1)} %get-tuple-element.21.north_ref, bf16[144,512]{1,0:T(8,128)(2,1)S(1)} %get-tuple-element.20.south_ref, bf16[512,1536]{1,0:T(8,128)(2,1)S(1)} %get-tuple-element.23.w_qkv_ref), custom_call_target="tpu_custom_call" | custom-call | tf_op jit(solution)/shard_map/pallas_call | solution.py:346
  7.2 0.1 collective-permute-start.3
  7.3 8.6 %collective-permute-start.4 = (bf16[144,512]{1,0:T(8,128)(2,1)S(1)}, bf16[144,512]{1,0:T(8,128)(2,1)S(1)}, u32[]{:S(2)}, u32[]{:S(2)}) collective-permute-start(bf16[144,512]{1,0:T(8,128)(2,1)S(1)} %get-tuple-element.25), channel_id=1, source_target_pairs={{1,2},{3,4},{5,6},{7,8},{9,10},{11,12},{13,14},{15,16},{17,18},{19... | collective-permute-start | bytes 442376 | tf_op jit(solution)/shard_map/ppermute | solution.py:369
  15.9 0.0 collective-permute-done.north_ref
  15.9 0.0 collective-permute-done.1.south_ref
  16.0 0.1 collective-permute-start.5
  16.1 5.9 %collective-permute-start.2 = (bf16[144,512]{1,0:T(8,128)(2,1)S(1)}, bf16[144,512]{1,0:T(8,128)(2,1)S(1)}, u32[]{:S(2)}, u32[]{:S(2)}) collective-permute-start(bf16[144,512]{1,0:T(8,128)(2,1)S(1)} %pad_maximum_fusion), channel_id=1, source_target_pairs={{1,2},{3,4},{5,6},{7,8},{9,10},{11,12},{13,14},{15,16},{17,18},{19... | collective-permute-start | bytes 442376 | tf_op jit(solution)/shard_map/ppermute | solution.py:369
  22.0 0.0 collective-permute-done.3.side_a_ref
  22.0 0.0 collective-permute-done.4.side_b_ref
  22.0 0.0 collective-permute-done.5.corner_ref
  22.0 3.7 %shard_map.156 = (bf16[144,512]{1,0:T(8,128)(2,1)S(1)}, f32[288,1024]{1,0:T(8,128)S(1)}, bf16[512,512]{1,0:T(8,128)(2,1)S(1)}, f32[1,512]{1,0:T(1,128)S(1)}, bf1...) custom-call(bf16[144,512]{1,0:T(8,128)(2,1)S(1)} %collective-permute-done.north_ref, ...), custom_call_target="tpu_custom_call" | custom-call | flops 99999997952 | tf_op jit(solution)/shard_map/pallas_call | solution.py:346
  25.7 0.0 collective-permute-done.2.corner_ref
  25.8 5.1 %shard_map.157 = bf16[18,4,1024]{2,1,0:T(4,128)(2,1)} custom-call(bf16[144,512]{1,0:T(8,128)(2,1)S(1)} %collective-permute-done.2.corner_ref, bf16[288,512]{1,0:T(8,128)(2,1)S(1)} %get-tuple-element.22.kept_ref, bf16[144,512]{1,0:T(8,128)(2,1)S(1)} %get-tuple-element.29.after_ref, f32[296,512]{1,0:T(8,128)S(1)} %get-tuple-element.26.query_ref, ...), custom_call_target="tpu_custom_call" | custom-call | tf_op jit(solution)/shard_map/pallas_call | solution.py:346
  (4 shorter events, 0.0 us)
Async XLA Ops:
  4.5 11.4 %collective-permute-start = (bf16[144,512]{1,0:T(8,128)(2,1)S(1)}, bf16[144,512]{1,0:T(8,128)(2,1)S(1)}, u32[]{:S(2)}, u32[]{:S(2)}) collective-permute-start(bf16[144,512]{1,0:T(8,128)(2,1)S(1)} %get-tuple-element.20.south_ref), channel_id=1, source_target_pairs={{224,0},{0,32},{32,64},{64,96},{96,128},{128,160},{160,192},{192,2... | collective-permute-start | bytes 442376 | tf_op jit(solution)/shard_map/ppermute | solution.py:363
  6.1 9.9 %collective-permute-start.1 = (bf16[144,512]{1,0:T(8,128)(2,1)S(1)}, bf16[144,512]{1,0:T(8,128)(2,1)S(1)}, u32[]{:S(2)}, u32[]{:S(2)}) collective-permute-start(bf16[144,512]{1,0:T(8,128)(2,1)S(1)} %get-tuple-element.21.north_ref), channel_id=1, source_target_pairs={{32,0},{64,32},{96,64},{128,96},{160,128},{192,160},{224,192},{0,2... | collective-permute-start | bytes 442376 | tf_op jit(solution)/shard_map/ppermute | solution.py:363
  7.2 14.8 %collective-permute-start.3 = (bf16[144,512]{1,0:T(8,128)(2,1)S(1)}, bf16[144,512]{1,0:T(8,128)(2,1)S(1)}, u32[]{:S(2)}, u32[]{:S(2)}) collective-permute-start(bf16[144,512]{1,0:T(8,128)(2,1)S(1)} %get-tuple-element.24), channel_id=1, source_target_pairs={{0,1},{2,3},{4,5},{6,7},{8,9},{10,11},{12,13},{14,15},{16,17},{18,... | collective-permute-start | bytes 442376 | tf_op jit(solution)/shard_map/ppermute | solution.py:369
  7.3 14.7 %collective-permute-start.4 = (bf16[144,512]{1,0:T(8,128)(2,1)S(1)}, bf16[144,512]{1,0:T(8,128)(2,1)S(1)}, u32[]{:S(2)}, u32[]{:S(2)}) collective-permute-start(bf16[144,512]{1,0:T(8,128)(2,1)S(1)} %get-tuple-element.25), channel_id=1, source_target_pairs={{1,2},{3,4},{5,6},{7,8},{9,10},{11,12},{13,14},{15,16},{17,18},{19... | collective-permute-start | bytes 442376 | tf_op jit(solution)/shard_map/ppermute | solution.py:369
  16.0 6.0 %collective-permute-start.5 = (bf16[144,512]{1,0:T(8,128)(2,1)S(1)}, bf16[144,512]{1,0:T(8,128)(2,1)S(1)}, u32[]{:S(2)}, u32[]{:S(2)}) collective-permute-start(bf16[144,512]{1,0:T(8,128)(2,1)S(1)} %pad_maximum_fusion.1), channel_id=1, source_target_pairs={{0,1},{2,3},{4,5},{6,7},{8,9},{10,11},{12,13},{14,15},{16,17},{18,... | collective-permute-start | bytes 442376 | tf_op jit(solution)/shard_map/ppermute | solution.py:369
  16.1 9.6 %collective-permute-start.2 = (bf16[144,512]{1,0:T(8,128)(2,1)S(1)}, bf16[144,512]{1,0:T(8,128)(2,1)S(1)}, u32[]{:S(2)}, u32[]{:S(2)}) collective-permute-start(bf16[144,512]{1,0:T(8,128)(2,1)S(1)} %pad_maximum_fusion), channel_id=1, source_target_pairs={{1,2},{3,4},{5,6},{7,8},{9,10},{11,12},{13,14},{15,16},{17,18},{19... | collective-permute-start | bytes 442376 | tf_op jit(solution)/shard_map/ppermute | solution.py:369
